TPU v7x, 32 devices: a whole 2x2x4 slice. The times are simulated.
32 devices in a mesh: groups: 2 (over x), seq: 8 (over z, y), tp: 2 (over core).
Axes of the slice: x: 2, y: 2, z: 4, core: 2. Of those that a mesh axis runs over, the one named last changes fastest.
Arguments:
- queries: bfloat16 [16384, 4096], P(('groups', 'seq'), 'tp'), parts along dimension 0, may hold values from -6 to 6
- keys: bfloat16 [16384, 4096], P(('groups', 'seq'), 'tp'), parts along dimension 0, may hold values from -6 to 6
- values: bfloat16 [16384, 4096], P(('groups', 'seq'), 'tp'), parts along dimension 0, may hold values from -6 to 6
- log_decay: float32 [16384, 32], P(('groups', 'seq'), 'tp'), parts along dimension 0, may hold values from -1 to 0, as said below
- gate: bfloat16 [16384, 4096], P(('groups', 'seq'), 'tp'), parts along dimension 0, may hold values from -6 to 6
- gain: bfloat16 [4096], P('tp'), may hold values from 0.099609375 to 1.8984375
- doc_lengths: int32 [16], P('groups'), parts along dimension 0, may hold values from 1 to 4096, 8192 in all
- owner_ids: int32 [16], P('groups'), parts along dimension 0, may hold values from 0 to 7, each once
Outputs:
- mixed: bfloat16 [16384, 4096], P(('groups', 'seq'), 'tp'), parts along dimension 0
- owner_states: bfloat16 [16, 32, 128, 128], P(('groups', 'seq'), 'tp'), parts along dimension 0
There are 2 independent parts, one for each index of `groups`. A program takes and returns all parts, laid end to end along the dimension named above; an argument that names none is the same for every part. Nothing has to cross between parts.
Inputs may be any that keep to these rules, and one draw needn't show every extreme that they name: `doc_lengths`: positive lengths summing to 8192; the longest prompt has exactly 4096 tokens. `owner_ids`: a permutation of the owner slots. `log_decay`: negative.
All inputs are finite; a program needn't handle non-finite values.
Results may differ from a plain program's by a relative error of at most 0.0049.
Values may be sent and summed in bfloat16 or wider, within the bound.
No kernel may reach another device: no remote copies, remote signals or barrier semaphores. Data moves between devices by JAX's collectives and lax.ppermute only.
A program may use at most 192 MiB of HBM per device.

v0:
```python
import functools
import math

import jax
import jax.numpy as jnp
from jax import lax
from jax.experimental import pallas as pl
from jax.experimental.pallas import tpu as pltpu
from jax.sharding import PartitionSpec as P

BLK = 512
SIDE = 3
EXTRA = 16
CHUNK = 256
MEMBERS = 4
TILE = 256
EARLY = (8,)
NEG = -1e30
LOG2E = math.log2(math.e)
SCALE = 128**-0.5
F32, BF16 = jnp.float32, jnp.bfloat16
SMEM = pl.BlockSpec(memory_space=pltpu.SMEM)
VMEM = pl.BlockSpec(memory_space=pltpu.VMEM)
LIMIT = pltpu.CompilerParams(vmem_limit_bytes=60 * 2**20)
SMALL = pltpu.CompilerParams(vmem_limit_bytes=48 * 2**20)


def dot(a, b, contract=((1,), (0,))):
    return lax.dot_general(a, b, (contract, ((), ())), preferred_element_type=F32)


def iota(shape, dim):
    return lax.broadcasted_iota(jnp.int32, shape, dim)


def read_ends(len_ref, count):
    ends, total = [], jnp.int32(0)
    for d in range(count):
        total = total + len_ref[d]
        ends.append(total)
    return ends


def run_end(ends, pos):
    best = ends[-1]
    for e in reversed(ends[:-1]):
        best = jnp.where(e > pos, e, best)
    return best


def run_start(ends, pos):
    best = jnp.zeros_like(pos)
    for e in ends[:-1]:
        best = jnp.where(e <= pos, e, best)
    return best


def split3(x):
    hi = x.astype(BF16)
    rest = x - hi.astype(F32)
    mid = rest.astype(BF16)
    return hi, mid, (rest - mid.astype(F32)).astype(BF16)


def cum_rows(ld_ref, crow_ref):
    heads, rows = ld_ref.shape
    upper = (iota((BLK, BLK), 0) <= iota((BLK, BLK), 1)).astype(F32).astype(BF16)
    base = jnp.zeros((heads, 1), F32)
    for b in range(rows // BLK):
        part = ld_ref[:, b * BLK : (b + 1) * BLK] * LOG2E
        sums = dot(jnp.concatenate(split3(part), axis=0), upper)
        row = sums[2 * heads :] + sums[heads : 2 * heads] + sums[:heads] + base
        crow_ref[:, b * BLK : (b + 1) * BLK] = row
        base = row[:, BLK - 1 :]


def value_at(cum, at, index):
    return jnp.sum(jnp.where(at == index, cum, 0.0), axis=1, keepdims=True)


def span_weights(cum, at, low, high):
    inside = (at >= low) & (at <= high)
    return jnp.exp2(jnp.where(inside, value_at(cum, at, high) - cum, NEG) + math.log2(SCALE))


def weigh(flipped, w_ref, h):
    weights = [jnp.broadcast_to(w_ref[pl.ds(h + j, 1), :], (128, flipped.shape[1])) for j in range(2)]
    return (flipped.astype(F32) * jnp.concatenate(weights, axis=0)).astype(BF16)


def whole(shape):
    return pl.BlockSpec(shape, lambda j: (0,) * len(shape))


def pieces_kernel(rest, len_ref, own_ref, ld_ref, k_ref, v_ref, *refs):
    if rest:
        side_ref, crow_ref, w_ref, keep_ref = refs
        slots = keep_ref.shape[0]
    else:
        crow_ref, flag_ref = refs[:2]
        side_refs, last_refs = refs[2 : 2 + MEMBERS], refs[2 + MEMBERS : 2 + 2 * MEMBERS]
        w_ref, first_ref, high_ref, weighted_ref, prefix_ref, parcel_ref = refs[2 + 2 * MEMBERS :]
        slots = SIDE
    heads, rows = crow_ref.shape
    step = pl.program_id(0)
    hp = v_ref.shape[1] // 128
    me = lax.axis_index("seq")

    @pl.when(step == 0)
    def _():
        cum_rows(ld_ref, crow_ref)
        first = me * rows
        last = first + rows - 1
        ends = read_ends(len_ref, len_ref.shape[0])
        starts = [jnp.int32(0)] + ends[:-1]
        lows = [jnp.int32(0)] * slots
        highs = [jnp.int32(-1)] * slots
        place, rank, previous = jnp.int32(0), jnp.int32(0), jnp.int32(-1)
        crowded, owned_in = jnp.int32(0), jnp.int32(0)
        for d in range(len(ends)):
            here = (ends[d] > first) & (ends[d] <= last)
            low = jnp.maximum(starts[d] - first, 0)
            for s in range(slots):
                mine = here & (place == s + (SIDE if rest else 0))
                lows[s] = jnp.where(mine, low, lows[s])
                highs[s] = jnp.where(mine, ends[d] - 1 - first, highs[s])
            place = place + here.astype(jnp.int32)
            device = (ends[d] - 1) // rows
            rank = jnp.where(device == previous, rank + 1, 0)
            previous = device
            late = ((rank >= SIDE) & (ends[d] != (device + 1) * rows)).astype(jnp.int32)
            crowded = jnp.maximum(crowded, late)
            owned_in = jnp.where(own_ref[d] == me, device, owned_in)
        at = iota((heads, rows), 1)
        cum = crow_ref[...]
        total = jnp.zeros((heads, rows), F32)
        for s in range(slots):
            total = total + span_weights(cum, at, lows[s], highs[s])
        if rest:
            row_at = iota((16, rows), 1)
            for s in range(slots):
                inside = (row_at >= lows[s]) & (row_at <= highs[s])
                keep_ref[s] = jnp.where(inside, 1.0, 0.0).astype(BF16)
        else:
            total = total + span_weights(cum, at, jnp.maximum(run_start(ends, last) - first, 0), rows - 1)
            flag_ref[0] = owned_in // MEMBERS
            flag_ref[1] = crowded
            high = jnp.int32(-1)
            for s in range(slots):
                high = jnp.maximum(high, highs[s])
                high_ref[s] = high
            stop = jnp.minimum(run_end(ends, first) - 1 - first, rows - 1)
            goes_on = (run_start(ends, first) < first).astype(F32)
            first_ref[...] = jnp.broadcast_to(jnp.exp2(value_at(cum, at, stop)) * goes_on, (heads, 128))
        w_ref[...] = total

    def own(states, j):
        return states[j * 128 : (j + 1) * 128, j * 128 : (j + 1) * 128]

    if rest:
        for i in range(0, hp, 2):
            lanes = slice(i * 128, (i + 2) * 128)
            weighted = weigh(k_ref[:, lanes].T, w_ref, step * hp + i).reshape(16, 16, rows)
            for s in range(slots):
                states = dot((weighted * keep_ref[s][None]).reshape(256, rows), v_ref[:, lanes])
                for j in range(2):
                    at = (s * hp + i + j) * 128
                    side_ref[0, at : at + 128, :] = own(states, j).astype(BF16)
        return

    pairs = range(0, hp, 2)
    lanes = {i: slice(i * 128, (i + 2) * 128) for i in pairs}
    for i in pairs:
        weighted_ref[lanes[i], :] = weigh(k_ref[:, lanes[i]].T, w_ref, step * hp + i)
    totals = {}
    for i in pairs:
        sums = [jnp.zeros((128, 128), F32)] * 2
        for t in range(rows // TILE):
            span = slice(t * TILE, (t + 1) * TILE)
            states = dot(weighted_ref[lanes[i], span], v_ref[span, lanes[i]])
            for j in range(2):
                prefix_ref[t, i + j] = sums[j]
                sums[j] = sums[j] + own(states, j)
        totals[i] = sums
    ended = {i: [jnp.zeros((128, 128), F32)] * 2 for i in pairs}
    for s in range(slots):
        high = high_ref[s]
        tile = jnp.maximum(high, 0) // TILE
        start = pl.multiple_of(tile * TILE, TILE)
        keep = jnp.where(start + iota((16, TILE), 1) <= high, 1.0, 0.0).astype(BF16)
        for i in pairs:
            kept = weighted_ref[lanes[i], pl.ds(start, TILE)].reshape(16, 16, TILE) * keep[None]
            states = dot(kept.reshape(256, TILE), v_ref[pl.ds(start, TILE), lanes[i]])
            for j in range(2):
                until = own(states, j) + prefix_ref[tile, i + j]
                at = (s * hp + i + j) * 128
                parcel_ref[at : at + 128, :] = (until - ended[i][j]).astype(BF16)
                ended[i][j] = until
    rate = first_ref[pl.ds(step * hp, hp), :]
    high = rate.astype(BF16).astype(F32)
    pad = jnp.zeros((EXTRA - 2 * hp, 128), F32)
    tail = jnp.concatenate([high, rate - high, pad], axis=0).astype(BF16)
    cut = SIDE * hp * 128
    for i in pairs:
        for j in range(2):
            at = cut + (i + j) * 128
            parcel_ref[at : at + 128, :] = (totals[i][j] - ended[i][j]).astype(BF16)
    parcel_ref[cut + hp * 128 :, :] = tail
    for x in range(MEMBERS):

        @pl.when((step ^ (me % MEMBERS)) == x)
        def _():
            side_refs[x][...] = parcel_ref[:cut, :]
            last_refs[x][...] = parcel_ref[cut:, :]


def piece_states(doc_lengths, owner_ids, decay_rows, keys, values, slots):
    heads, rows = decay_rows.shape
    rest = slots > SIDE
    count = slots - SIDE if rest else slots
    hp = heads // MEMBERS
    wide = pl.BlockSpec((rows, hp * 128), lambda j: (0, j))
    side = (count * hp * 128, 128)
    shapes, specs = [jax.ShapeDtypeStruct((heads, rows), F32)], [whole((heads, rows))]
    scratch = [pltpu.VMEM((heads, rows), F32)]
    if rest:
        shapes.insert(0, jax.ShapeDtypeStruct((MEMBERS,) + side, BF16))
        specs.insert(0, pl.BlockSpec((1,) + side, lambda j: (j, 0, 0)))
        scratch.append(pltpu.VMEM((count, 16, rows), BF16))
    else:
        last = (hp * 128 + EXTRA, 128)
        shapes += [jax.ShapeDtypeStruct((2,), jnp.int32)]
        shapes += [jax.ShapeDtypeStruct(shape, BF16) for shape in (side, last) for _ in range(MEMBERS)]
        specs += [SMEM] + [whole(shape) for shape in (side, last) for _ in range(MEMBERS)]
        scratch += [
            pltpu.VMEM((heads, 128), F32),
            pltpu.SMEM((SIDE,), jnp.int32),
            pltpu.VMEM((hp * 128, rows), BF16),
            pltpu.VMEM((rows // TILE, hp, 128, 128), F32),
            pltpu.VMEM((side[0] + last[0], 128), BF16),
        ]
    return pl.pallas_call(
        functools.partial(pieces_kernel, rest),
        grid=(MEMBERS,),
        in_specs=[SMEM, SMEM, whole((heads, rows)), wide, wide],
        out_specs=specs,
        out_shape=shapes,
        scratch_shapes=scratch,
        compiler_params=LIMIT,
        cost_estimate=pl.CostEstimate(
            flops=2 * heads * rows * 128 * 256, bytes_accessed=rows * heads * 128 * 4, transcendentals=heads * rows
        ),
        name="piece_states",
    )(doc_lengths, owner_ids, decay_rows, keys, values)


def head_column(ccol_ref, h):
    cols = ccol_ref[...]
    return jnp.sum(jnp.where(iota(cols.shape, 1) == h, cols, 0.0), axis=1, keepdims=True)


def fill_columns(crow_ref, ccol_ref):
    heads, rows = crow_ref.shape
    for r0 in range(0, rows, 128):
        part = crow_ref[:, r0 : r0 + 128]
        part = jnp.concatenate([part, jnp.zeros((128 - heads, 128), F32)], axis=0)
        ccol_ref[r0 : r0 + 128, :] = part.T


def fill_bias(first, ends, bias_ref):
    for c in range(bias_ref.shape[0] // CHUNK):
        base = first + c * CHUNK
        t_pos = base + iota((CHUNK, 1), 0)
        start = run_start(ends, t_pos)
        s_pos = base + iota((CHUNK, CHUNK), 1)
        keep = (s_pos <= t_pos) & (s_pos >= start)
        bias_ref[c * CHUNK : (c + 1) * CHUNK, :] = jnp.where(keep, math.log2(SCALE), NEG)


def attend(first, ends, q_ref, k_ref, v_ref, h, crow_ref, ccol_ref, bias_ref, states, emit):
    rows = q_ref.shape[0]
    pair = range(2)
    half = CHUNK // 2
    lanes = [slice(i * 128, (i + 1) * 128) for i in pair]
    row_all = [crow_ref[pl.ds(h + i, 1), :] for i in pair]
    col_all = [head_column(ccol_ref, h + i) for i in pair]
    starts = range(0, rows, CHUNK)
    spans = [slice(r0, r0 + CHUNK) for r0 in starts]
    reach = [run_end(ends, first + r0 - 1) - (first + r0) for r0 in starts]
    base = [[row_all[i][:, r0 - 1 : r0] if r0 else jnp.zeros((1, 1), F32) for r0 in starts] for i in pair]

    fresh = [[], []]
    for c, r0 in enumerate(starts[:-1]):
        since = run_start(ends, first + r0 + CHUNK - 1) - (first + r0)
        inside = iota((1, CHUNK), 1) >= since
        for i in pair:
            row = row_all[i][:, spans[c]]
            weight = jnp.exp2(jnp.where(inside, row[:, CHUNK - 1 :] - row, NEG) + math.log2(SCALE))
            flipped = k_ref[spans[c], lanes[i]].T
            fresh[i].append(dot((flipped.astype(F32) * weight).astype(BF16), v_ref[spans[c], lanes[i]]))
    carried = []
    for i in pair:
        state = None if states is None else states[i]
        chain = [None if state is None else state.astype(BF16)]
        for c in range(len(starts) - 1):
            if state is None:
                state = fresh[i][c]
            else:
                total = row_all[i][:, starts[c] + CHUNK - 1 : starts[c] + CHUNK]
                state = fresh[i][c] + state * jnp.exp2(jnp.where(CHUNK <= reach[c], total - base[i][c], NEG))
            chain.append(state.astype(BF16))
        carried.append(chain)

    def products(c):
        result = []
        for i in pair:
            query = q_ref[spans[c], lanes[i]]
            scores = dot(query, k_ref[spans[c], lanes[i]], ((1,), (1,)))
            result.append((scores, None if carried[i][c] is None else dot(query, carried[i][c])))
        return result

    ahead = products(0)
    for c, r0 in enumerate(starts):
        current = ahead
        if c + 1 < len(starts):
            ahead = products(c + 1)
        for part in range(2):
            t0, width = part * half, (part + 1) * half
            rows_here = slice(r0 + t0, r0 + t0 + half)
            for i in pair:
                scores, carry = current[i]
                col = col_all[i][rows_here]
                decay = jnp.exp2((col - row_all[i][:, r0 : r0 + width]) + bias_ref[rows_here, :width])
                weights = (scores[t0 : t0 + half, :width] * decay).astype(BF16)
                att = dot(weights, v_ref[r0 : r0 + width, lanes[i]])
                if carry is not None:
                    lead = jnp.exp2(jnp.where(t0 + iota((half, 1), 0) < reach[c], col - base[i][c], NEG))
                    att = att + lead * carry[t0 : t0 + half]
                emit(lanes[i], r0 + t0, half, att)


def early_kernel(pairs_before, len_ref, q_ref, k_ref, v_ref, crow_ref, *refs):
    out_ref, bias_ref, ccol_ref = refs[-3:]
    rows = q_ref.shape[0]
    step = pl.program_id(0)
    first = lax.axis_index("seq") * rows
    ends = read_ends(len_ref, len_ref.shape[0])

    @pl.when(step == 0)
    def _():
        fill_bias(first, ends, bias_ref)
        fill_columns(crow_ref, ccol_ref)

    def emit(lanes, t0, size, att):
        out_ref[t0 : t0 + size, lanes] = att

    attend(first, ends, q_ref, k_ref, v_ref, (step + pairs_before) * 2, crow_ref, ccol_ref, bias_ref, None, emit)


def early_attention(doc_lengths, queries, keys, values, crow, before, part):
    heads, rows = crow.shape
    skip = sum(EARLY[:part]) // 2
    wide = pl.BlockSpec((rows, 256), lambda j: (0, j + skip))
    count = EARLY[part]
    return pl.pallas_call(
        functools.partial(early_kernel, skip),
        grid=(count // 2,),
        in_specs=[SMEM, wide, wide, wide, whole((heads, rows))] + [pl.BlockSpec(memory_space=pl.ANY)] * len(before),
        out_specs=wide,
        out_shape=jax.ShapeDtypeStruct((rows, sum(EARLY) * 128), F32),
        input_output_aliases={5: 0} if before else {},
        scratch_shapes=[pltpu.VMEM((rows, CHUNK), F32), pltpu.VMEM((rows, 128), F32)],
        compiler_params=LIMIT,
        cost_estimate=pl.CostEstimate(
            flops=count * rows * CHUNK * 128 * 8, bytes_accessed=rows * count * 128 * 10, transcendentals=count * rows * CHUNK
        ),
        name="early_attention",
    )(doc_lengths, queries, keys, values, crow, *before)


def gather_last(refs, last_ref):
    me = lax.axis_index("seq") % MEMBERS
    for x, ref in enumerate(refs):
        last_ref[me ^ x] = ref[...]


def decay_of(last_ref, e, i, hp):
    extra = last_ref[e, hp * 128 :, :].astype(F32)
    return extra[i : i + 1, :] + extra[hp + i : hp + i + 1, :]


def scan_quad(rows, len_ref, last_ref, state, i, hp, note):
    members = last_ref.shape[0]
    ends = read_ends(len_ref, len_ref.shape[0])
    base = lax.axis_index("seq") // members * members
    for e in range(members):
        note(e, state)
        low = (base + e) * rows
        inner = jnp.int32(0)
        for end in ends:
            inner = inner + ((end > low) & (end < low + rows)).astype(jnp.int32)
        passes = (inner == 0).astype(F32)
        piece = last_ref[e, i * 128 : (i + 1) * 128, :].astype(F32)
        state = state * (decay_of(last_ref, e, i, hp) * passes) + piece
    return state


def leave_kernel(rows, len_ref, *refs):
    out_ref, last_ref = refs[-2:]
    gather_last(refs[:MEMBERS], last_ref)
    hp = out_ref.shape[0]
    for i in range(hp):
        state = jnp.zeros((128, 128), F32)
        if len(refs) > MEMBERS + 2:
            state = refs[MEMBERS][i].astype(F32)
        state = scan_quad(rows, len_ref, last_ref, state, i, hp, lambda e, x: None)
        out_ref[i] = state.astype(BF16)


def leave_quad(doc_lengths, last, coming, rows, hp):
    return pl.pallas_call(
        functools.partial(leave_kernel, rows),
        in_specs=[SMEM] + [VMEM] * (MEMBERS + len(coming)),
        out_specs=VMEM,
        out_shape=jax.ShapeDtypeStruct((hp, 128, 128), BF16),
        scratch_shapes=[pltpu.VMEM((MEMBERS,) + last[0].shape, BF16)],
        compiler_params=SMALL,
        name="leave_quad",
    )(doc_lengths, *last, *coming)


def enter_kernel(rows, len_ref, *refs):
    in_ref, out_refs, last_ref, state_ref = refs[MEMBERS], refs[MEMBERS + 1 : -2], refs[-2], refs[-1]
    gather_last(refs[:MEMBERS], last_ref)
    hp = in_ref.shape[0]

    def note(i, e, state):
        state_ref[e, i] = state

    for i in range(hp):
        scan_quad(rows, len_ref, last_ref, in_ref[i].astype(F32), i, hp, functools.partial(note, i))
    me = lax.axis_index("seq") % MEMBERS
    for x, out_ref in enumerate(out_refs):
        out_ref[...] = state_ref[me ^ x].astype(BF16)


def enter_states(doc_lengths, last, coming, rows):
    return pl.pallas_call(
        functools.partial(enter_kernel, rows),
        in_specs=[SMEM] + [VMEM] * (MEMBERS + 1),
        out_specs=[VMEM] * MEMBERS,
        out_shape=[jax.ShapeDtypeStruct(coming.shape, BF16)] * MEMBERS,
        scratch_shapes=[
            pltpu.VMEM((MEMBERS,) + last[0].shape, BF16),
            pltpu.VMEM((MEMBERS,) + coming.shape, F32),
        ],
        compiler_params=SMALL,
        name="enter_states",
    )(doc_lengths, *last, coming)


def final_kernel(rows, len_ref, own_ref, *refs):
    side_refs = refs[MEMBERS : 2 * MEMBERS]
    rest_ref, in_ref = refs[2 * MEMBERS : 2 * MEMBERS + 2]
    out_refs, (last_ref, state_ref, piece_ref, final_ref) = refs[2 * MEMBERS + 2 : -4], refs[-4:]
    gather_last(refs[:MEMBERS], last_ref)
    hp = in_ref.shape[0]
    ends = read_ends(len_ref, len_ref.shape[0])
    me = lax.axis_index("seq")
    base = me // MEMBERS * MEMBERS

    def note(i, e, state):
        state_ref[e, i] = state

    for i in range(hp):
        scan_quad(rows, len_ref, last_ref, in_ref[i].astype(F32), i, hp, functools.partial(note, i))
    final_ref[...] = jnp.zeros_like(final_ref)
    place, previous = jnp.int32(0), jnp.int32(-1)
    for d in range(len(ends)):
        device = (ends[d] - 1) // rows
        place = jnp.where(device == previous, place + 1, 0)
        previous = device
        at_end = ends[d] == (device + 1) * rows
        enters = (place == 0).astype(F32)
        mine = device // MEMBERS * MEMBERS == base
        inner = mine & jnp.logical_not(at_end)
        e = device - base

        @pl.when(mine & at_end)
        def _():
            piece_ref[...] = last_ref[e, : hp * 128, :]

        for x, side_ref in enumerate(side_refs):

            @pl.when(inner & (place < SIDE) & ((e ^ (me % MEMBERS)) == x))
            def _():
                piece_ref[...] = side_ref[pl.ds(pl.multiple_of(place * hp * 128, 128), hp * 128), :]

        @pl.when(inner & (place >= SIDE))
        def _():
            row = pl.multiple_of((place - SIDE) * hp * 128, 128)
            pltpu.sync_copy(rest_ref.at[e, pl.ds(row, hp * 128), :], piece_ref)

        @pl.when(mine)
        def _():
            for i in range(hp):
                local = piece_ref[i * 128 : (i + 1) * 128, :].astype(F32)
                state = local + state_ref[e, i] * (decay_of(last_ref, e, i, hp) * enters)
                final_ref[own_ref[d], i] = state.astype(BF16)

    for x, out_ref in enumerate(out_refs):
        out_ref[...] = final_ref[me ^ x]


def final_states(doc_lengths, owner_ids, last, side, rest, coming, rows, spread):
    return pl.pallas_call(
        functools.partial(final_kernel, rows),
        in_specs=[SMEM, SMEM] + [VMEM] * (2 * MEMBERS) + [pl.BlockSpec(memory_space=pl.ANY), VMEM],
        out_specs=[VMEM] * spread,
        out_shape=[jax.ShapeDtypeStruct(coming.shape, BF16)] * spread,
        scratch_shapes=[
            pltpu.VMEM((MEMBERS,) + last[0].shape, BF16),
            pltpu.VMEM((MEMBERS,) + coming.shape, F32),
            pltpu.VMEM((coming.shape[0] * 128, 128), BF16),
            pltpu.VMEM((spread,) + coming.shape, BF16),
        ],
        compiler_params=SMALL,
        name="final_states",
    )(doc_lengths, owner_ids, *last, *side, rest, coming)


def pick_kernel(flag_ref, *refs):
    in_refs, out_ref = refs[:-1], refs[-1]
    me = lax.axis_index("seq")
    hp = in_refs[0].shape[0]
    for x, ref in enumerate(in_refs):
        source = me ^ x

        @pl.when(source // MEMBERS == flag_ref[0])
        def _():
            out_ref[0, pl.ds(source % MEMBERS * hp, hp)] = ref[...]


def pick_owned(flags, arrived, heads):
    return pl.pallas_call(
        pick_kernel,
        in_specs=[SMEM] + [VMEM] * len(arrived),
        out_specs=VMEM,
        out_shape=jax.ShapeDtypeStruct((1, heads, 128, 128), BF16),
        compiler_params=SMALL,
        name="pick_owned",
    )(flags, *arrived)


def finish_kernel(
    len_ref, q_ref, k_ref, v_ref, e0, e1, e2, e3, local_ref, gate_ref, gain_ref, crow_ref, out_ref, bias_ref, ccol_ref
):
    rows = q_ref.shape[0]
    step = pl.program_id(0)
    me = lax.axis_index("seq")
    first = me * rows
    ends = read_ends(len_ref, len_ref.shape[0])
    hp = e0.shape[0]
    pairs = sum(EARLY) // 2

    def entering(h):
        far = (h // hp) ^ (me % MEMBERS)
        state = e0[h % hp]
        for x, ref in ((1, e1), (2, e2), (3, e3)):
            state = jnp.where(far == x, ref[h % hp], state)
        return state

    def emit(lanes, t0, size, att):
        mean = jnp.mean(att * att, axis=1, keepdims=True)
        gate = 0.5 + 0.5 * jnp.tanh(0.5 * gate_ref[t0 : t0 + size, lanes].astype(F32))
        gain = gain_ref[:, lanes].astype(F32)
        out_ref[t0 : t0 + size, lanes] = (att * lax.rsqrt(mean + 1e-06) * (gain * gate)).astype(BF16)

    @pl.when(step == 0)
    def _():
        fill_bias(first, ends, bias_ref)
        fill_columns(crow_ref, ccol_ref)

    @pl.when(step < pairs)
    def _():
        reach = run_end(ends, first - 1) - first
        cols = [head_column(ccol_ref, step * 2 + i) for i in range(2)]
        states = [entering(step * 2 + i) for i in range(2)]
        lanes = [slice(i * 128, (i + 1) * 128) for i in range(2)]
        for t0 in range(0, rows, 256):
            carry = [dot(q_ref[t0 : t0 + 256, lanes[i]], states[i]) for i in range(2)]
            at = t0 + iota((256, 1), 0)
            for i in range(2):
                lead = jnp.exp2(jnp.where(at < reach, cols[i][t0 : t0 + 256], NEG))
                emit(lanes[i], t0, 256, local_ref[t0 : t0 + 256, lanes[i]] + lead * carry[i])

    @pl.when(step >= pairs)
    def _():
        states = [entering(step * 2 + i).astype(F32) for i in range(2)]
        attend(first, ends, q_ref, k_ref, v_ref, step * 2, crow_ref, ccol_ref, bias_ref, states, emit)


def finish(doc_lengths, queries, keys, values, entering, local, gate, gain, crow):
    heads, rows = crow.shape
    pairs = sum(EARLY) // 2
    wide = pl.BlockSpec((rows, 256), lambda j: (0, j))
    late = pl.BlockSpec((rows, 256), lambda j: (0, jnp.maximum(j, pairs)))
    return pl.pallas_call(
        finish_kernel,
        grid=(heads // 2,),
        in_specs=[SMEM, wide, late, late]
        + [whole(e.shape) for e in entering]
        + [
            pl.BlockSpec((rows, 256), lambda j: (0, jnp.minimum(j, pairs - 1))),
            wide,
            pl.BlockSpec((1, 256), lambda j: (0, j)),
            whole((heads, rows)),
        ],
        out_specs=wide,
        out_shape=jax.ShapeDtypeStruct((rows, heads * 128), BF16),
        scratch_shapes=[pltpu.VMEM((rows, CHUNK), F32), pltpu.VMEM((rows, 128), F32)],
        compiler_params=LIMIT,
        cost_estimate=pl.CostEstimate(
            flops=heads * rows * CHUNK * 128 * 8, bytes_accessed=rows * heads * 128 * 10, transcendentals=heads * rows * CHUNK
        ),
        name="finish",
    )(doc_lengths, queries, keys, values, *entering, local, gate, gain, crow)


def swap(x, groups=None):
    return lax.all_to_all(x, "seq", split_axis=0, concat_axis=0, axis_index_groups=groups, tiled=True)


def by_distance(parcels, spread):
    moved = {0: parcels[0]}
    for x in sorted(range(1, len(parcels)), key=lambda x: (x < MEMBERS, x)):
        moved[x] = lax.ppermute(parcels[x], "seq", [(s, s ^ x) for s in range(spread)])
    return [moved[x] for x in range(len(parcels))]


def on_device(spread, queries, keys, values, log_decay, gate, gain, doc_lengths, owner_ids):
    rows, heads = log_decay.shape
    quads = spread // MEMBERS
    hp = heads // MEMBERS
    near = [[q * MEMBERS + m for m in range(MEMBERS)] for q in range(quads)]
    onward = [(s, s + MEMBERS) for s in range(spread - MEMBERS)]
    decay_rows = log_decay.T
    barrier = lax.optimization_barrier

    crow, flags, *parcels = piece_states(doc_lengths, owner_ids, decay_rows, keys, values, SIDE)
    side, last = parcels[:MEMBERS], parcels[MEMBERS:]
    last = by_distance(last, spread)
    gain = gain.reshape(1, -1)
    crowded = flags[1] > 0
    slots = max(doc_lengths.shape[0] - 1, SIDE + 1)

    def send_rest():
        return swap(piece_states(doc_lengths, owner_ids, decay_rows, keys, values, slots)[0], near)

    none = jnp.zeros((MEMBERS, (slots - SIDE) * hp * 128, 128), BF16)
    rest = lax.cond(crowded, send_rest, lambda: none)
    last, side, gain, rest = barrier((last, side, gain, rest))

    side = by_distance(side, spread)
    coming = []
    for _ in range(quads - 1):
        leaving = leave_quad(doc_lengths, last, coming, rows, hp)
        coming = [lax.ppermute(leaving, "seq", onward)]
    crow_1, leaving = barrier((crow, leaving))
    local = early_attention(doc_lengths, queries, keys, values, crow_1, [], 0)
    coming, local, side = barrier((coming[0], local, side))

    entering = by_distance(enter_states(doc_lengths, last, coming, rows), spread)
    finals = final_states(doc_lengths, owner_ids, last, side, rest, coming, rows, spread)
    entering, finals = barrier((entering, finals))
    arrived = by_distance(finals, spread)
    mixed = finish(doc_lengths, queries, keys, values, entering, local, gate, gain, crow)
    return mixed, pick_owned(flags, arrived, heads)


def solution(mesh):
    placed = (
        P(("groups", "seq"), "tp"),
        P(("groups", "seq"), "tp"),
        P(("groups", "seq"), "tp"),
        P(("groups", "seq"), "tp"),
        P(("groups", "seq"), "tp"),
        P("tp"),
        P("groups"),
        P("groups"),
    )
    return jax.shard_map(
        functools.partial(on_device, mesh.shape["seq"]),
        mesh=mesh,
        in_specs=placed,
        out_specs=(P(("groups", "seq"), "tp"), P(("groups", "seq"), "tp", None, None)),
        check_vma=False,
    )
```

profile of v0, /device:TPU:0, one launch (start us, length us, event | category | flops | bytes accessed | tf_op | source)
XLA Modules:
  0.0 85.6 jit_solution(4671976057308109811)
XLA Ops:
  0.7 8.1 %piece_states.3 = (f32[16,1024]{1,0:T(8,128)}, s32[2]{0:T(128)}, bf16[1536,128]{1,0:T(8,128)(2,1)}, bf16[1536,128]{1,0:T(8,128)(2,1)}, bf16[1536,128]{1,0:T(8,12...) custom-call(s32[8]{0:T(128)} %len_ref.11, ...), custom_call_target="tpu_custom_call" | custom-call | flops 1073741824 | bytes 8388608 | tf_op jit(solution)/shard_map/piece_states/pallas_call | solution.py:242
  8.8 3.0 %collective-permute-start = (bf16[528,128]{1,0:T(8,128)(2,1)}, bf16[528,128]{1,0:T(8,128)(2,1)S(1)}, u32[]{:S(2)}, u32[]{:S(2)}) collective-permute-start(bf16[528,128]{1,0:T(8,128)(2,1)} %get-tuple-element.73), channel_id=1, source_target_pairs={{0,2},{2,0},{4,6},{6,4},{8,10},{10,8},{12,14},{14,12},{1,3},{3,1},... | collective-permute-start | bytes 405512 | tf_op jit(solution)/shard_map/ppermute | solution.py:637
  11.8 1.6 %collective-permute-start.1 = (bf16[528,128]{1,0:T(8,128)(2,1)}, bf16[528,128]{1,0:T(8,128)(2,1)S(1)}, u32[]{:S(2)}, u32[]{:S(2)}) collective-permute-start(bf16[528,128]{1,0:T(8,128)(2,1)} %get-tuple-element.74), channel_id=1, source_target_pairs={{0,4},{2,6},{4,0},{6,2},{8,12},{10,14},{12,8},{14,10},{1,5},{3,7},... | collective-permute-start | bytes 405512 | tf_op jit(solution)/shard_map/ppermute | solution.py:637
  13.4 0.0 collective-permute-start.2
  13.4 1.2 %slice.3 = s32[1]{0:T(128)} slice(s32[2]{0:T(128)} %get-tuple-element.80.flag_ref), slice={[1:2]} | slice | bytes 8 | tf_op jit(solution)/shard_map/slice | solution.py:654
  15.2 0.6 reshape.11.gain_ref
  15.9 0.3 conditional.1
  15.9 0.3 broadcast_in_dim.2
  16.2 0.0 copy-start.4
  16.2 0.0 collective-permute-done.refs_1_
  16.2 2.3 %collective-permute-done.1.refs_2_ = bf16[528,128]{1,0:T(8,128)(2,1)S(1)} collective-permute-done((bf16[528,128]{1,0:T(8,128)(2,1)}, bf16[528,128]{1,0:T(8,128)(2,1)S(1)}, u32[]{:S(2)}, u32[]{:S(2)}) %collective-permute-start.1) | collective-permute-done | bytes 135200 | tf_op jit(solution)/shard_map/ppermute | solution.py:637
  18.5 1.3 %collective-permute-done.2.refs_3_ = bf16[528,128]{1,0:T(8,128)(2,1)S(1)} collective-permute-done((bf16[528,128]{1,0:T(8,128)(2,1)}, bf16[528,128]{1,0:T(8,128)(2,1)S(1)}, u32[]{:S(2)}, u32[]{:S(2)}) %collective-permute-start.2) | collective-permute-done | bytes 135200 | tf_op jit(solution)/shard_map/ppermute | solution.py:637
  19.8 1.7 %collective-permute-start.4 = (bf16[1536,128]{1,0:T(8,128)(2,1)}, bf16[1536,128]{1,0:T(8,128)(2,1)S(1)}, u32[]{:S(2)}, u32[]{:S(2)}) collective-permute-start(bf16[1536,128]{1,0:T(8,128)(2,1)} %get-tuple-element.88), channel_id=1, source_target_pairs={{0,2},{2,0},{4,6},{6,4},{8,10},{10,8},{12,14},{14,12},{1,3},{3,1},... | collective-permute-start | bytes 1179656 | tf_op jit(solution)/shard_map/ppermute | solution.py:637
  21.4 1.6 %collective-permute-start.5 = (bf16[1536,128]{1,0:T(8,128)(2,1)}, bf16[1536,128]{1,0:T(8,128)(2,1)S(1)}, u32[]{:S(2)}, u32[]{:S(2)}) collective-permute-start(bf16[1536,128]{1,0:T(8,128)(2,1)} %get-tuple-element.89), channel_id=1, source_target_pairs={{0,4},{2,6},{4,0},{6,2},{8,12},{10,14},{12,8},{14,10},{1,5},{3,7},... | collective-permute-start | bytes 1179656 | tf_op jit(solution)/shard_map/ppermute | solution.py:637
  23.0 0.2 collective-permute-start.6
  23.3 0.7 leave_quad.1
  24.0 4.7 %collective-permute-start.3 = (bf16[4,128,128]{2,1,0:T(8,128)(2,1)S(1)}, bf16[4,128,128]{2,1,0:T(8,128)(2,1)S(1)}, u32[]{:S(2)}, u32[]{:S(2)}) collective-permute-start(bf16[4,128,128]{2,1,0:T(8,128)(2,1)S(1)} %leave_quad.1), channel_id=1, source_target_pairs={{0,8},{2,10},{4,12},{6,14},{1,9},{3,11},{5,13},{7,15},{16,24},{18,... | collective-permute-start | bytes 393224 | tf_op jit(solution)/shard_map/ppermute | solution.py:668
  28.6 0.0 copy-start.1
  28.7 8.1 %early_attention.1.local_ref = f32[1024,1024]{1,0:T(8,128)} custom-call(s32[8]{0:T(128)S(1)} %copy-done.9, bf16[1024,2048]{1,0:T(8,128)(2,1)} %q_ref.3, bf16[1024,2048]{1,0:T(8,128)(2,1)} %k_ref.5, bf16[1024,2048]{1,0:T(8,128)(2,1)} %v_ref.5, f32[16,1024]{1,0:T(8,128)} %get-tuple-element.86.crow_ref), custom_call_target="tpu_custom_call" | custom-call | flops 2147483648 | bytes 10485760 | tf_op jit(solution)/shard_map/early_attention/pallas_call | solution.py:365
  36.8 5.2 %collective-permute-done.3.refs_4_.refs_9_ = bf16[4,128,128]{2,1,0:T(8,128)(2,1)S(1)} collective-permute-done((bf16[4,128,128]{2,1,0:T(8,128)(2,1)S(1)}, bf16[4,128,128]{2,1,0:T(8,128)(2,1)S(1)}, u32[]{:S(2)}, u32[]{:S(2)}) %collective-permute-start.3) | collective-permute-done | bytes 131104 | tf_op jit(solution)/shard_map/ppermute | solution.py:668
  42.0 0.0 collective-permute-done.4.refs_5_
  42.0 0.0 collective-permute-done.5.refs_6_
  42.0 0.0 collective-permute-done.6.refs_7_
  42.1 0.8 enter_states.1
  42.8 0.1 collective-permute-start.7
  42.9 1.6 %collective-permute-start.8 = (bf16[4,128,128]{2,1,0:T(8,128)(2,1)S(1)}, bf16[4,128,128]{2,1,0:T(8,128)(2,1)S(1)}, u32[]{:S(2)}, u32[]{:S(2)}) collective-permute-start(bf16[4,128,128]{2,1,0:T(8,128)(2,1)S(1)} %get-tuple-element.94), channel_id=1, source_target_pairs={{0,4},{2,6},{4,0},{6,2},{8,12},{10,14},{12,8},{14,10},{1,5},{3,7},... | collective-permute-start | bytes 393224 | tf_op jit(solution)/shard_map/ppermute | solution.py:637
  44.5 1.8 %collective-permute-start.9 = (bf16[4,128,128]{2,1,0:T(8,128)(2,1)S(1)}, bf16[4,128,128]{2,1,0:T(8,128)(2,1)S(1)}, u32[]{:S(2)}, u32[]{:S(2)}) collective-permute-start(bf16[4,128,128]{2,1,0:T(8,128)(2,1)S(1)} %get-tuple-element.95), channel_id=1, source_target_pairs={{0,6},{2,4},{4,2},{6,0},{8,14},{10,12},{12,10},{14,8},{1,7},{3,5},... | collective-permute-start | bytes 393224 | tf_op jit(solution)/shard_map/ppermute | solution.py:637
  46.4 1.6 %final_states.1 = (bf16[4,128,128]{2,1,0:T(8,128)(2,1)S(1)}, bf16[4,128,128]{2,1,0:T(8,128)(2,1)S(1)}, bf16[4,128,128]{2,1,0:T(8,128)(2,1)S(1)}, bf16[4,128,128]...) custom-call(s32[8]{0:T(128)S(1)} %copy-done.9, ...), custom_call_target="tpu_custom_call" | custom-call | tf_op jit(solution)/shard_map/final_states/pallas_call | solution.py:516
  48.0 0.0 collective-permute-done.7.e1
  48.0 0.0 copy-start.6
  48.0 0.0 collective-permute-done.8.e2
  48.1 4.1 %collective-permute-done.9.e3 = bf16[4,128,128]{2,1,0:T(8,128)(2,1)S(1)} collective-permute-done((bf16[4,128,128]{2,1,0:T(8,128)(2,1)S(1)}, bf16[4,128,128]{2,1,0:T(8,128)(2,1)S(1)}, u32[]{:S(2)}, u32[]{:S(2)}) %collective-permute-start.9) | collective-permute-done | bytes 131104 | tf_op jit(solution)/shard_map/ppermute | solution.py:637
  52.2 0.0 collective-permute-start.10
  52.2 2.1 %collective-permute-start.11 = (bf16[4,128,128]{2,1,0:T(8,128)(2,1)S(1)}, bf16[4,128,128]{2,1,0:T(8,128)(2,1)S(1)}, u32[]{:S(2)}, u32[]{:S(2)}) collective-permute-start(bf16[4,128,128]{2,1,0:T(8,128)(2,1)S(1)} %get-tuple-element.117), channel_id=1, source_target_pairs={{0,4},{2,6},{4,0},{6,2},{8,12},{10,14},{12,8},{14,10},{1,5},{3,7},... | collective-permute-start | bytes 393224 | tf_op jit(solution)/shard_map/ppermute | solution.py:637
  54.2 1.4 %collective-permute-start.12 = (bf16[4,128,128]{2,1,0:T(8,128)(2,1)S(1)}, bf16[4,128,128]{2,1,0:T(8,128)(2,1)S(1)}, u32[]{:S(2)}, u32[]{:S(2)}) collective-permute-start(bf16[4,128,128]{2,1,0:T(8,128)(2,1)S(1)} %get-tuple-element.118), channel_id=1, source_target_pairs={{0,6},{2,4},{4,2},{6,0},{8,14},{10,12},{12,10},{14,8},{1,7},{3,5},... | collective-permute-start | bytes 393224 | tf_op jit(solution)/shard_map/ppermute | solution.py:637
  55.6 3.0 %collective-permute-start.13 = (bf16[4,128,128]{2,1,0:T(8,128)(2,1)S(1)}, bf16[4,128,128]{2,1,0:T(8,128)(2,1)S(1)}, u32[]{:S(2)}, u32[]{:S(2)}) collective-permute-start(bf16[4,128,128]{2,1,0:T(8,128)(2,1)S(1)} %get-tuple-element.119), channel_id=1, source_target_pairs={{0,8},{2,10},{4,12},{6,14},{8,0},{10,2},{12,4},{14,6},{1,9},{3,11}... | collective-permute-start | bytes 393224 | tf_op jit(solution)/shard_map/ppermute | solution.py:637
  58.6 0.0 collective-permute-start.14
  58.6 0.0 collective-permute-done.10.refs_1_
  58.6 3.4 %collective-permute-start.15 = (bf16[4,128,128]{2,1,0:T(8,128)(2,1)S(1)}, bf16[4,128,128]{2,1,0:T(8,128)(2,1)S(1)}, u32[]{:S(2)}, u32[]{:S(2)}) collective-permute-start(bf16[4,128,128]{2,1,0:T(8,128)(2,1)S(1)} %get-tuple-element.121), channel_id=1, source_target_pairs={{0,12},{2,14},{4,8},{6,10},{8,4},{10,6},{12,0},{14,2},{1,13},{3,15... | collective-permute-start | bytes 393224 | tf_op jit(solution)/shard_map/ppermute | solution.py:637
  62.0 0.0 collective-permute-done.11.refs_2_
  62.0 4.4 %collective-permute-start.16 = (bf16[4,128,128]{2,1,0:T(8,128)(2,1)S(1)}, bf16[4,128,128]{2,1,0:T(8,128)(2,1)S(1)}, u32[]{:S(2)}, u32[]{:S(2)}) collective-permute-start(bf16[4,128,128]{2,1,0:T(8,128)(2,1)S(1)} %get-tuple-element.122), channel_id=1, source_target_pairs={{0,14},{2,12},{4,10},{6,8},{8,6},{10,4},{12,2},{14,0},{1,15},{3,13... | collective-permute-start | bytes 393224 | tf_op jit(solution)/shard_map/ppermute | solution.py:637
  66.4 17.7 %finish.1 = bf16[1024,2048]{1,0:T(8,128)(2,1)} custom-call(s32[8]{0:T(128)S(1)} %copy-done.9, bf16[1024,2048]{1,0:T(8,128)(2,1)} %q_ref.3, bf16[1024,2048]{1,0:T(8,128)(2,1)} %k_ref.5, bf16[1024,2048]{1,0:T(8,128)(2,1)} %v_ref.5, bf16[4,128,128]{2,1,0:T(8,128)(2,1)} %copy-done.2, bf16[4,128,128]{2,1,0:T(8,128)(2,1)} %copy-done.6, ...), custom_call_target="tpu_custom_call" | custom-call | flops 4294967296 | bytes 20971520 | tf_op jit(solution)/shard_map/finish/pallas_call | solution.py:608
  84.1 0.0 collective-permute-done.12.refs_3_
  84.1 0.0 collective-permute-done.13.refs_4_
  84.1 0.0 collective-permute-done.14.refs_5_
  84.1 0.0 collective-permute-done.15.refs_6_
  84.1 0.0 collective-permute-done.16.refs_7_
  84.1 1.5 %pick_owned.1 = bf16[1,16,128,128]{3,2,1,0:T(8,128)(2,1)} custom-call(s32[2]{0:T(128)S(1)} %copy-done.3, bf16[4,128,128]{2,1,0:T(8,128)(2,1)S(1)} %get-tuple-element.115.refs_0_, bf16[4,128,128]{2,1,0:T(8,128)(2,1)S(1)} %collective-permute-done.10.refs_1_, bf16[4,128,128]{2,1,0:T(8,128)(2,1)S(1)} %collective-permute-done.11.refs_2_, ...), custom_call_target="tpu_custom_call" | custom-call | tf_op jit(solution)/shard_map/pick_owned/pallas_call | solution.py:545
  (23 shorter events, 0.0 us)
Async XLA Ops:
  0.6 14.6 %copy-start.11 = (bf16[2048]{0:T(1024)(128)(2,1)S(1)}, bf16[2048]{0:T(1024)(128)(2,1)}, u32[]{:S(2)}) copy-start(bf16[2048]{0:T(1024)(128)(2,1)} %param.15) | copy-start | bytes 12292
  0.6 15.2 %copy-start.5 = (f32[1024,16]{0,1:T(8,128)S(1)}, f32[1024,16]{0,1:T(8,128)}, u32[]{:S(2)}) copy-start(f32[1024,16]{0,1:T(8,128)} %param.13) | copy-start | bytes 196612
  0.7 15.2 %copy-start.9 = (s32[8]{0:T(128)S(1)}, s32[8]{0:T(128)}, u32[]{:S(2)}) copy-start(s32[8]{0:T(128)} %len_ref.11) | copy-start | bytes 100
  0.7 15.2 %copy-start.10 = (s32[8]{0:T(128)S(1)}, s32[8]{0:T(128)}, u32[]{:S(2)}) copy-start(s32[8]{0:T(128)} %own_ref.3) | copy-start | bytes 100
  8.8 7.4 %collective-permute-start = (bf16[528,128]{1,0:T(8,128)(2,1)}, bf16[528,128]{1,0:T(8,128)(2,1)S(1)}, u32[]{:S(2)}, u32[]{:S(2)}) collective-permute-start(bf16[528,128]{1,0:T(8,128)(2,1)} %get-tuple-element.73), channel_id=1, source_target_pairs={{0,2},{2,0},{4,6},{6,4},{8,10},{10,8},{12,14},{14,12},{1,3},{3,1},... | collective-permute-start | bytes 405512 | tf_op jit(solution)/shard_map/ppermute | solution.py:637
  11.8 6.7 %collective-permute-start.1 = (bf16[528,128]{1,0:T(8,128)(2,1)}, bf16[528,128]{1,0:T(8,128)(2,1)S(1)}, u32[]{:S(2)}, u32[]{:S(2)}) collective-permute-start(bf16[528,128]{1,0:T(8,128)(2,1)} %get-tuple-element.74), channel_id=1, source_target_pairs={{0,4},{2,6},{4,0},{6,2},{8,12},{10,14},{12,8},{14,10},{1,5},{3,7},... | collective-permute-start | bytes 405512 | tf_op jit(solution)/shard_map/ppermute | solution.py:637
  13.4 6.4 %collective-permute-start.2 = (bf16[528,128]{1,0:T(8,128)(2,1)}, bf16[528,128]{1,0:T(8,128)(2,1)S(1)}, u32[]{:S(2)}, u32[]{:S(2)}) collective-permute-start(bf16[528,128]{1,0:T(8,128)(2,1)} %get-tuple-element.75), channel_id=1, source_target_pairs={{0,6},{2,4},{4,2},{6,0},{8,14},{10,12},{12,10},{14,8},{1,7},{3,5},... | collective-permute-start | bytes 405512 | tf_op jit(solution)/shard_map/ppermute | solution.py:637
  15.9 7.2 %copy-start.12 = (bf16[1536,128]{1,0:T(8,128)(2,1)S(1)}, bf16[1536,128]{1,0:T(8,128)(2,1)}, u32[]{:S(2)}) copy-start(bf16[1536,128]{1,0:T(8,128)(2,1)} %get-tuple-element.90) | copy-start | bytes 1179652
  15.9 7.4 %copy-start = (bf16[528,128]{1,0:T(8,128)(2,1)S(1)}, bf16[528,128]{1,0:T(8,128)(2,1)}, u32[]{:S(2)}) copy-start(bf16[528,128]{1,0:T(8,128)(2,1)} %get-tuple-element.81.refs_0_) | copy-start | bytes 405508
  16.2 3.6 %copy-start.4 = (bf16[4,2048,128]{2,1,0:T(8,128)(2,1)}, bf16[4,2048,128]{2,1,0:T(8,128)(2,1)S(1)}, u32[]{:S(2)}) copy-start(bf16[4,2048,128]{2,1,0:T(8,128)(2,1)S(1)} %get-tuple-element.123.refs_8_) | copy-start | bytes 6291460
  19.8 22.3 %collective-permute-start.4 = (bf16[1536,128]{1,0:T(8,128)(2,1)}, bf16[1536,128]{1,0:T(8,128)(2,1)S(1)}, u32[]{:S(2)}, u32[]{:S(2)}) collective-permute-start(bf16[1536,128]{1,0:T(8,128)(2,1)} %get-tuple-element.88), channel_id=1, source_target_pairs={{0,2},{2,0},{4,6},{6,4},{8,10},{10,8},{12,14},{14,12},{1,3},{3,1},... | collective-permute-start | bytes 1179656 | tf_op jit(solution)/shard_map/ppermute | solution.py:637
  21.4 20.6 %collective-permute-start.5 = (bf16[1536,128]{1,0:T(8,128)(2,1)}, bf16[1536,128]{1,0:T(8,128)(2,1)S(1)}, u32[]{:S(2)}, u32[]{:S(2)}) collective-permute-start(bf16[1536,128]{1,0:T(8,128)(2,1)} %get-tuple-element.89), channel_id=1, source_target_pairs={{0,4},{2,6},{4,0},{6,2},{8,12},{10,14},{12,8},{14,10},{1,5},{3,7},... | collective-permute-start | bytes 1179656 | tf_op jit(solution)/shard_map/ppermute | solution.py:637
  23.0 19.0 %collective-permute-start.6 = (bf16[1536,128]{1,0:T(8,128)(2,1)S(1)}, bf16[1536,128]{1,0:T(8,128)(2,1)S(1)}, u32[]{:S(2)}, u32[]{:S(2)}) collective-permute-start(bf16[1536,128]{1,0:T(8,128)(2,1)S(1)} %copy-done.12), channel_id=1, source_target_pairs={{0,6},{2,4},{4,2},{6,0},{8,14},{10,12},{12,10},{14,8},{1,7},{3,5},... | collective-permute-start | bytes 1179656 | tf_op jit(solution)/shard_map/ppermute | solution.py:637
  24.0 18.1 %collective-permute-start.3 = (bf16[4,128,128]{2,1,0:T(8,128)(2,1)S(1)}, bf16[4,128,128]{2,1,0:T(8,128)(2,1)S(1)}, u32[]{:S(2)}, u32[]{:S(2)}) collective-permute-start(bf16[4,128,128]{2,1,0:T(8,128)(2,1)S(1)} %leave_quad.1), channel_id=1, source_target_pairs={{0,8},{2,10},{4,12},{6,14},{1,9},{3,11},{5,13},{7,15},{16,24},{18,... | collective-permute-start | bytes 393224 | tf_op jit(solution)/shard_map/ppermute | solution.py:668
  28.6 17.8 %copy-start.1 = (bf16[1536,128]{1,0:T(8,128)(2,1)S(1)}, bf16[1536,128]{1,0:T(8,128)(2,1)}, u32[]{:S(2)}) copy-start(bf16[1536,128]{1,0:T(8,128)(2,1)} %get-tuple-element.96.refs_4_) | copy-start | bytes 1179652
  42.8 5.2 %copy-start.2 = (bf16[4,128,128]{2,1,0:T(8,128)(2,1)}, bf16[4,128,128]{2,1,0:T(8,128)(2,1)S(1)}, u32[]{:S(2)}) copy-start(bf16[4,128,128]{2,1,0:T(8,128)(2,1)S(1)} %get-tuple-element.109.e0) | copy-start | bytes 393220
  42.8 5.2 %collective-permute-start.7 = (bf16[4,128,128]{2,1,0:T(8,128)(2,1)S(1)}, bf16[4,128,128]{2,1,0:T(8,128)(2,1)S(1)}, u32[]{:S(2)}, u32[]{:S(2)}) collective-permute-start(bf16[4,128,128]{2,1,0:T(8,128)(2,1)S(1)} %get-tuple-element.93), channel_id=1, source_target_pairs={{0,2},{2,0},{4,6},{6,4},{8,10},{10,8},{12,14},{14,12},{1,3},{3,1},... | collective-permute-start | bytes 393224 | tf_op jit(solution)/shard_map/ppermute | solution.py:637
  42.9 5.1 %collective-permute-start.8 = (bf16[4,128,128]{2,1,0:T(8,128)(2,1)S(1)}, bf16[4,128,128]{2,1,0:T(8,128)(2,1)S(1)}, u32[]{:S(2)}, u32[]{:S(2)}) collective-permute-start(bf16[4,128,128]{2,1,0:T(8,128)(2,1)S(1)} %get-tuple-element.94), channel_id=1, source_target_pairs={{0,4},{2,6},{4,0},{6,2},{8,12},{10,14},{12,8},{14,10},{1,5},{3,7},... | collective-permute-start | bytes 393224 | tf_op jit(solution)/shard_map/ppermute | solution.py:637
  44.5 7.6 %collective-permute-start.9 = (bf16[4,128,128]{2,1,0:T(8,128)(2,1)S(1)}, bf16[4,128,128]{2,1,0:T(8,128)(2,1)S(1)}, u32[]{:S(2)}, u32[]{:S(2)}) collective-permute-start(bf16[4,128,128]{2,1,0:T(8,128)(2,1)S(1)} %get-tuple-element.95), channel_id=1, source_target_pairs={{0,6},{2,4},{4,2},{6,0},{8,14},{10,12},{12,10},{14,8},{1,7},{3,5},... | collective-permute-start | bytes 393224 | tf_op jit(solution)/shard_map/ppermute | solution.py:637
  48.0 18.4 %copy-start.6 = (bf16[4,128,128]{2,1,0:T(8,128)(2,1)}, bf16[4,128,128]{2,1,0:T(8,128)(2,1)S(1)}, u32[]{:S(2)}) copy-start(bf16[4,128,128]{2,1,0:T(8,128)(2,1)S(1)} %collective-permute-done.7.e1) | copy-start | bytes 393220
  48.1 18.4 %copy-start.7 = (bf16[4,128,128]{2,1,0:T(8,128)(2,1)}, bf16[4,128,128]{2,1,0:T(8,128)(2,1)S(1)}, u32[]{:S(2)}) copy-start(bf16[4,128,128]{2,1,0:T(8,128)(2,1)S(1)} %collective-permute-done.8.e2) | copy-start | bytes 393220
  52.2 14.3 %copy-start.8 = (bf16[4,128,128]{2,1,0:T(8,128)(2,1)}, bf16[4,128,128]{2,1,0:T(8,128)(2,1)S(1)}, u32[]{:S(2)}) copy-start(bf16[4,128,128]{2,1,0:T(8,128)(2,1)S(1)} %collective-permute-done.9.e3) | copy-start | bytes 393220
  52.2 32.0 %copy-start.3 = (s32[2]{0:T(128)S(1)}, s32[2]{0:T(128)}, u32[]{:S(2)}) copy-start(s32[2]{0:T(128)} %get-tuple-element.80.flag_ref) | copy-start | bytes 28
  52.2 6.5 %collective-permute-start.10 = (bf16[4,128,128]{2,1,0:T(8,128)(2,1)S(1)}, bf16[4,128,128]{2,1,0:T(8,128)(2,1)S(1)}, u32[]{:S(2)}, u32[]{:S(2)}) collective-permute-start(bf16[4,128,128]{2,1,0:T(8,128)(2,1)S(1)} %get-tuple-element.116), channel_id=1, source_target_pairs={{0,2},{2,0},{4,6},{6,4},{8,10},{10,8},{12,14},{14,12},{1,3},{3,1},... | collective-permute-start | bytes 393224 | tf_op jit(solution)/shard_map/ppermute | solution.py:637
  52.2 9.9 %collective-permute-start.11 = (bf16[4,128,128]{2,1,0:T(8,128)(2,1)S(1)}, bf16[4,128,128]{2,1,0:T(8,128)(2,1)S(1)}, u32[]{:S(2)}, u32[]{:S(2)}) collective-permute-start(bf16[4,128,128]{2,1,0:T(8,128)(2,1)S(1)} %get-tuple-element.117), channel_id=1, source_target_pairs={{0,4},{2,6},{4,0},{6,2},{8,12},{10,14},{12,8},{14,10},{1,5},{3,7},... | collective-permute-start | bytes 393224 | tf_op jit(solution)/shard_map/ppermute | solution.py:637
  54.2 29.9 %collective-permute-start.12 = (bf16[4,128,128]{2,1,0:T(8,128)(2,1)S(1)}, bf16[4,128,128]{2,1,0:T(8,128)(2,1)S(1)}, u32[]{:S(2)}, u32[]{:S(2)}) collective-permute-start(bf16[4,128,128]{2,1,0:T(8,128)(2,1)S(1)} %get-tuple-element.118), channel_id=1, source_target_pairs={{0,6},{2,4},{4,2},{6,0},{8,14},{10,12},{12,10},{14,8},{1,7},{3,5},... | collective-permute-start | bytes 393224 | tf_op jit(solution)/shard_map/ppermute | solution.py:637
  55.6 28.4 %collective-permute-start.13 = (bf16[4,128,128]{2,1,0:T(8,128)(2,1)S(1)}, bf16[4,128,128]{2,1,0:T(8,128)(2,1)S(1)}, u32[]{:S(2)}, u32[]{:S(2)}) collective-permute-start(bf16[4,128,128]{2,1,0:T(8,128)(2,1)S(1)} %get-tuple-element.119), channel_id=1, source_target_pairs={{0,8},{2,10},{4,12},{6,14},{8,0},{10,2},{12,4},{14,6},{1,9},{3,11}... | collective-permute-start | bytes 393224 | tf_op jit(solution)/shard_map/ppermute | solution.py:637
  58.6 25.5 %collective-permute-start.14 = (bf16[4,128,128]{2,1,0:T(8,128)(2,1)S(1)}, bf16[4,128,128]{2,1,0:T(8,128)(2,1)S(1)}, u32[]{:S(2)}, u32[]{:S(2)}) collective-permute-start(bf16[4,128,128]{2,1,0:T(8,128)(2,1)S(1)} %get-tuple-element.120), channel_id=1, source_target_pairs={{0,10},{2,8},{4,14},{6,12},{8,2},{10,0},{12,6},{14,4},{1,11},{3,9}... | collective-permute-start | bytes 393224 | tf_op jit(solution)/shard_map/ppermute | solution.py:637
  58.6 25.5 %collective-permute-start.15 = (bf16[4,128,128]{2,1,0:T(8,128)(2,1)S(1)}, bf16[4,128,128]{2,1,0:T(8,128)(2,1)S(1)}, u32[]{:S(2)}, u32[]{:S(2)}) collective-permute-start(bf16[4,128,128]{2,1,0:T(8,128)(2,1)S(1)} %get-tuple-element.121), channel_id=1, source_target_pairs={{0,12},{2,14},{4,8},{6,10},{8,4},{10,6},{12,0},{14,2},{1,13},{3,15... | collective-permute-start | bytes 393224 | tf_op jit(solution)/shard_map/ppermute | solution.py:637
  62.0 22.1 %collective-permute-start.16 = (bf16[4,128,128]{2,1,0:T(8,128)(2,1)S(1)}, bf16[4,128,128]{2,1,0:T(8,128)(2,1)S(1)}, u32[]{:S(2)}, u32[]{:S(2)}) collective-permute-start(bf16[4,128,128]{2,1,0:T(8,128)(2,1)S(1)} %get-tuple-element.122), channel_id=1, source_target_pairs={{0,14},{2,12},{4,10},{6,8},{8,6},{10,4},{12,2},{14,0},{1,15},{3,13... | collective-permute-start | bytes 393224 | tf_op jit(solution)/shard_map/ppermute | solution.py:637
where the time goes:
time: 86 us; the launch traced here: 85.6 us
  Pallas kernels  38.5 us (45%)
  starting transfers between devices  30.6 us (36%)
  waiting for transfers between devices  12.9 us (15%)
  local copies, waits for them, and re-layouts  2.12 us (2%)
  between operations  1.52 us (2%)
    ppermute x16, starting transfers between devices, by_distance(): lax.ppermute(parcels[x], 'seq', [(s, s ^ x) for s in range(spread)])  25.9 us
    pallas_call x1, Pallas kernels, finish(): pl.pallas_call(finish_kernel, grid=(heads // 2,), in_specs=[SMEM, wide, l...  17.7 us
    pallas_call x1, Pallas kernels, early_attention(): pl.pallas_call(functools.partial(early_kernel, skip), grid=(count // 2,),...  8.15 us
    pallas_call x1, Pallas kernels, piece_states(): pl.pallas_call(functools.partial(pieces_kernel, rest), grid=(MEMBERS,), i...  8.07 us
    ppermute x16, waiting for transfers between devices, by_distance(): lax.ppermute(parcels[x], 'seq', [(s, s ^ x) for s in range(spread)])  7.68 us
    ppermute x1, waiting for transfers between devices, on_device(): coming = [lax.ppermute(leaving, 'seq', onward)]  5.24 us
    ppermute x1, starting transfers between devices, on_device(): coming = [lax.ppermute(leaving, 'seq', onward)]  4.66 us
  transfers between devices with their start and end apart: 17, of which 4 were waited for; matrix products, arithmetic and copies ran while one was open for 2% of the time, Pallas kernels for 33%

commit v1 on v0

--- a/solution.py
+++ b/solution.py
@@ -14,7 +14,6 @@
 CHUNK = 256
 MEMBERS = 4
 TILE = 256
-EARLY = (8,)
 NEG = -1e30
 LOG2E = math.log2(math.e)
 SCALE = 128**-0.5
@@ -277,7 +276,7 @@
         bias_ref[c * CHUNK : (c + 1) * CHUNK, :] = jnp.where(keep, math.log2(SCALE), NEG)
 
 
-def attend(first, ends, q_ref, k_ref, v_ref, h, crow_ref, ccol_ref, bias_ref, states, emit):
+def attend(first, ends, q_ref, k_ref, v_ref, h, crow_ref, ccol_ref, bias_ref, out_ref):
     rows = q_ref.shape[0]
     pair = range(2)
     half = CHUNK // 2
@@ -287,7 +286,7 @@
     starts = range(0, rows, CHUNK)
     spans = [slice(r0, r0 + CHUNK) for r0 in starts]
     reach = [run_end(ends, first + r0 - 1) - (first + r0) for r0 in starts]
-    base = [[row_all[i][:, r0 - 1 : r0] if r0 else jnp.zeros((1, 1), F32) for r0 in starts] for i in pair]
+    base = [[row_all[i][:, r0 - 1 : r0] if r0 else None for r0 in starts] for i in pair]
 
     fresh = [[], []]
     for c, r0 in enumerate(starts[:-1]):
@@ -300,14 +299,11 @@
             fresh[i].append(dot((flipped.astype(F32) * weight).astype(BF16), v_ref[spans[c], lanes[i]]))
     carried = []
     for i in pair:
-        state = None if states is None else states[i]
-        chain = [None if state is None else state.astype(BF16)]
-        for c in range(len(starts) - 1):
-            if state is None:
-                state = fresh[i][c]
-            else:
-                total = row_all[i][:, starts[c] + CHUNK - 1 : starts[c] + CHUNK]
-                state = fresh[i][c] + state * jnp.exp2(jnp.where(CHUNK <= reach[c], total - base[i][c], NEG))
+        state = fresh[i][0]
+        chain = [None, state.astype(BF16)]
+        for c in range(1, len(starts) - 1):
+            total = row_all[i][:, starts[c] + CHUNK - 1 : starts[c] + CHUNK]
+            state = fresh[i][c] + state * jnp.exp2(jnp.where(CHUNK <= reach[c], total - base[i][c], NEG))
             chain.append(state.astype(BF16))
         carried.append(chain)
 
@@ -316,7 +312,7 @@
         for i in pair:
             query = q_ref[spans[c], lanes[i]]
             scores = dot(query, k_ref[spans[c], lanes[i]], ((1,), (1,)))
-            result.append((scores, None if carried[i][c] is None else dot(query, carried[i][c])))
+            result.append((scores, dot(query, carried[i][c]) if c else None))
         return result
 
     ahead = products(0)
@@ -333,14 +329,13 @@
                 decay = jnp.exp2((col - row_all[i][:, r0 : r0 + width]) + bias_ref[rows_here, :width])
                 weights = (scores[t0 : t0 + half, :width] * decay).astype(BF16)
                 att = dot(weights, v_ref[r0 : r0 + width, lanes[i]])
-                if carry is not None:
+                if c:
                     lead = jnp.exp2(jnp.where(t0 + iota((half, 1), 0) < reach[c], col - base[i][c], NEG))
                     att = att + lead * carry[t0 : t0 + half]
-                emit(lanes[i], r0 + t0, half, att)
-
-
-def early_kernel(pairs_before, len_ref, q_ref, k_ref, v_ref, crow_ref, *refs):
-    out_ref, bias_ref, ccol_ref = refs[-3:]
+                out_ref[rows_here, lanes[i]] = att
+
+
+def local_kernel(len_ref, q_ref, k_ref, v_ref, crow_ref, out_ref, bias_ref, ccol_ref):
     rows = q_ref.shape[0]
     step = pl.program_id(0)
     first = lax.axis_index("seq") * rows
@@ -351,31 +346,25 @@
         fill_bias(first, ends, bias_ref)
         fill_columns(crow_ref, ccol_ref)
 
-    def emit(lanes, t0, size, att):
-        out_ref[t0 : t0 + size, lanes] = att
-
-    attend(first, ends, q_ref, k_ref, v_ref, (step + pairs_before) * 2, crow_ref, ccol_ref, bias_ref, None, emit)
-
-
-def early_attention(doc_lengths, queries, keys, values, crow, before, part):
+    attend(first, ends, q_ref, k_ref, v_ref, step * 2, crow_ref, ccol_ref, bias_ref, out_ref)
+
+
+def local_attention(doc_lengths, queries, keys, values, crow):
     heads, rows = crow.shape
-    skip = sum(EARLY[:part]) // 2
-    wide = pl.BlockSpec((rows, 256), lambda j: (0, j + skip))
-    count = EARLY[part]
+    wide = pl.BlockSpec((rows, 256), lambda j: (0, j))
     return pl.pallas_call(
-        functools.partial(early_kernel, skip),
-        grid=(count // 2,),
-        in_specs=[SMEM, wide, wide, wide, whole((heads, rows))] + [pl.BlockSpec(memory_space=pl.ANY)] * len(before),
+        local_kernel,
+        grid=(heads // 2,),
+        in_specs=[SMEM, wide, wide, wide, whole((heads, rows))],
         out_specs=wide,
-        out_shape=jax.ShapeDtypeStruct((rows, sum(EARLY) * 128), F32),
-        input_output_aliases={5: 0} if before else {},
+        out_shape=jax.ShapeDtypeStruct((rows, heads * 128), F32),
         scratch_shapes=[pltpu.VMEM((rows, CHUNK), F32), pltpu.VMEM((rows, 128), F32)],
         compiler_params=LIMIT,
         cost_estimate=pl.CostEstimate(
-            flops=count * rows * CHUNK * 128 * 8, bytes_accessed=rows * count * 128 * 10, transcendentals=count * rows * CHUNK
+            flops=heads * rows * CHUNK * 128 * 8, bytes_accessed=rows * heads * 128 * 10, transcendentals=heads * rows * CHUNK
         ),
-        name="early_attention",
-    )(doc_lengths, queries, keys, values, crow, *before)
+        name="local_attention",
+    )(doc_lengths, queries, keys, values, crow)
 
 
 def gather_last(refs, last_ref):
@@ -552,16 +541,15 @@
     )(flags, *arrived)
 
 
-def finish_kernel(
-    len_ref, q_ref, k_ref, v_ref, e0, e1, e2, e3, local_ref, gate_ref, gain_ref, crow_ref, out_ref, bias_ref, ccol_ref
-):
+def finish_kernel(len_ref, q_ref, e0, e1, e2, e3, local_ref, gate_ref, gain_ref, crow_ref, out_ref, ccol_ref):
     rows = q_ref.shape[0]
     step = pl.program_id(0)
     me = lax.axis_index("seq")
-    first = me * rows
-    ends = read_ends(len_ref, len_ref.shape[0])
     hp = e0.shape[0]
-    pairs = sum(EARLY) // 2
+
+    @pl.when(step == 0)
+    def _():
+        fill_columns(crow_ref, ccol_ref)
 
     def entering(h):
         far = (h // hp) ^ (me % MEMBERS)
@@ -570,61 +558,42 @@
             state = jnp.where(far == x, ref[h % hp], state)
         return state
 
-    def emit(lanes, t0, size, att):
-        mean = jnp.mean(att * att, axis=1, keepdims=True)
-        gate = 0.5 + 0.5 * jnp.tanh(0.5 * gate_ref[t0 : t0 + size, lanes].astype(F32))
-        gain = gain_ref[:, lanes].astype(F32)
-        out_ref[t0 : t0 + size, lanes] = (att * lax.rsqrt(mean + 1e-06) * (gain * gate)).astype(BF16)
-
-    @pl.when(step == 0)
-    def _():
-        fill_bias(first, ends, bias_ref)
-        fill_columns(crow_ref, ccol_ref)
-
-    @pl.when(step < pairs)
-    def _():
-        reach = run_end(ends, first - 1) - first
-        cols = [head_column(ccol_ref, step * 2 + i) for i in range(2)]
-        states = [entering(step * 2 + i) for i in range(2)]
-        lanes = [slice(i * 128, (i + 1) * 128) for i in range(2)]
-        for t0 in range(0, rows, 256):
-            carry = [dot(q_ref[t0 : t0 + 256, lanes[i]], states[i]) for i in range(2)]
-            at = t0 + iota((256, 1), 0)
-            for i in range(2):
-                lead = jnp.exp2(jnp.where(at < reach, cols[i][t0 : t0 + 256], NEG))
-                emit(lanes[i], t0, 256, local_ref[t0 : t0 + 256, lanes[i]] + lead * carry[i])
-
-    @pl.when(step >= pairs)
-    def _():
-        states = [entering(step * 2 + i).astype(F32) for i in range(2)]
-        attend(first, ends, q_ref, k_ref, v_ref, step * 2, crow_ref, ccol_ref, bias_ref, states, emit)
-
-
-def finish(doc_lengths, queries, keys, values, entering, local, gate, gain, crow):
+    first = me * rows
+    reach = run_end(read_ends(len_ref, len_ref.shape[0]), first - 1) - first
+    cols = [head_column(ccol_ref, step * 2 + i) for i in range(2)]
+    states = [entering(step * 2 + i) for i in range(2)]
+    for t0 in range(0, rows, 256):
+        span = slice(t0, t0 + 256)
+        carry = [dot(q_ref[span, i * 128 : (i + 1) * 128], states[i]) for i in range(2)]
+        inside = t0 + iota((256, 1), 0) < reach
+        for i in range(2):
+            lanes = slice(i * 128, (i + 1) * 128)
+            lead = jnp.exp2(jnp.where(inside, cols[i][span], NEG))
+            att = local_ref[span, lanes] + lead * carry[i]
+            mean = jnp.mean(att * att, axis=1, keepdims=True)
+            gate = 0.5 + 0.5 * jnp.tanh(0.5 * gate_ref[span, lanes].astype(F32))
+            gain = gain_ref[:, lanes].astype(F32)
+            out_ref[span, lanes] = (att * lax.rsqrt(mean + 1e-06) * (gain * gate)).astype(BF16)
+
+
+def finish(doc_lengths, queries, entering, local, gate, gain, crow):
     heads, rows = crow.shape
-    pairs = sum(EARLY) // 2
     wide = pl.BlockSpec((rows, 256), lambda j: (0, j))
-    late = pl.BlockSpec((rows, 256), lambda j: (0, jnp.maximum(j, pairs)))
     return pl.pallas_call(
         finish_kernel,
         grid=(heads // 2,),
-        in_specs=[SMEM, wide, late, late]
+        in_specs=[SMEM, wide]
         + [whole(e.shape) for e in entering]
-        + [
-            pl.BlockSpec((rows, 256), lambda j: (0, jnp.minimum(j, pairs - 1))),
-            wide,
-            pl.BlockSpec((1, 256), lambda j: (0, j)),
-            whole((heads, rows)),
-        ],
+        + [wide, wide, pl.BlockSpec((1, 256), lambda j: (0, j)), whole((heads, rows))],
         out_specs=wide,
         out_shape=jax.ShapeDtypeStruct((rows, heads * 128), BF16),
-        scratch_shapes=[pltpu.VMEM((rows, CHUNK), F32), pltpu.VMEM((rows, 128), F32)],
-        compiler_params=LIMIT,
+        scratch_shapes=[pltpu.VMEM((rows, 128), F32)],
+        compiler_params=pltpu.CompilerParams(vmem_limit_bytes=54 * 2**20),
         cost_estimate=pl.CostEstimate(
-            flops=heads * rows * CHUNK * 128 * 8, bytes_accessed=rows * heads * 128 * 10, transcendentals=heads * rows * CHUNK
+            flops=heads * rows * 128 * 256, bytes_accessed=rows * heads * 128 * 10, transcendentals=heads * rows * 256
         ),
         name="finish",
-    )(doc_lengths, queries, keys, values, *entering, local, gate, gain, crow)
+    )(doc_lengths, queries, *entering, local, gate, gain, crow)
 
 
 def swap(x, groups=None):
@@ -667,14 +636,14 @@
         leaving = leave_quad(doc_lengths, last, coming, rows, hp)
         coming = [lax.ppermute(leaving, "seq", onward)]
     crow_1, leaving = barrier((crow, leaving))
-    local = early_attention(doc_lengths, queries, keys, values, crow_1, [], 0)
+    local = local_attention(doc_lengths, queries, keys, values, crow_1)
     coming, local, side = barrier((coming[0], local, side))
 
     entering = by_distance(enter_states(doc_lengths, last, coming, rows), spread)
     finals = final_states(doc_lengths, owner_ids, last, side, rest, coming, rows, spread)
     entering, finals = barrier((entering, finals))
     arrived = by_distance(finals, spread)
-    mixed = finish(doc_lengths, queries, keys, values, entering, local, gate, gain, crow)
+    mixed = finish(doc_lengths, queries, entering, local, gate, gain, crow)
     return mixed, pick_owned(flags, arrived, heads)
 
 

time: 86 us -> 81.6 us (0.949)
  waiting for transfers between devices: 12.9 us -> 9.71 us
  starting transfers between devices: 30.6 us -> 27.9 us
  Pallas kernels: 38.5 us -> 39.7 us
    ppermute x1, waiting for transfers between devices: 5.24 us -> 0.01 us  [on_device(): coming = [lax.ppermute(leaving, 'seq', onward)]]
    ppermute x16, starting transfers between devices: 25.9 us -> 23.2 us  [by_distance(): lax.ppermute(parcels[x], 'seq', [(s, s ^ x) for s in range(spread)])]
    ppermute x16, waiting for transfers between devices: 7.68 us -> 9.71 us  [by_distance(): lax.ppermute(parcels[x], 'seq', [(s, s ^ x) for s in range(spread)])]
    pallas_call x2, Pallas kernels: 25.8 us -> 27.1 us  [the longest x1 14 us: local_attention(): pl.pallas_call(local_kernel, grid=(heads // 2,), in_specs=[SMEM, wide, wi...]
  transfers between devices with their start and end apart: 17 -> 17, of which waited for: 4 -> 5; matrix products, arithmetic and copies ran while one was open for 2% -> 3% of each run, Pallas kernels for 33% -> 35%
where the time goes in v1:
time: 81.6 us; the launch traced here: 81 us
  Pallas kernels  39.7 us (49%)
  starting transfers between devices  27.9 us (34%)
  waiting for transfers between devices  9.71 us (12%)
  local copies, waits for them, and re-layouts  2.18 us (3%)
  between operations  1.52 us (2%)
    ppermute x16, starting transfers between devices, by_distance(): lax.ppermute(parcels[x], 'seq', [(s, s ^ x) for s in range(spread)])  23.2 us
    pallas_call x1, Pallas kernels, local_attention(): pl.pallas_call(local_kernel, grid=(heads // 2,), in_specs=[SMEM, wide, wi...  14 us
    pallas_call x1, Pallas kernels, finish(): pl.pallas_call(finish_kernel, grid=(heads // 2,), in_specs=[SMEM, wide] +...  13.1 us
    ppermute x16, waiting for transfers between devices, by_distance(): lax.ppermute(parcels[x], 'seq', [(s, s ^ x) for s in range(spread)])  9.71 us
    pallas_call x1, Pallas kernels, piece_states(): pl.pallas_call(functools.partial(pieces_kernel, rest), grid=(MEMBERS,), i...  8.16 us
    ppermute x1, starting transfers between devices, on_device(): coming = [lax.ppermute(leaving, 'seq', onward)]  4.67 us
  transfers between devices with their start and end apart: 17, of which 5 were waited for; matrix products, arithmetic and copies ran while one was open for 3% of the time, Pallas kernels for 35%

profile of v1, /device:TPU:0, one launch (start us, length us, event | category | flops | bytes accessed | tf_op | source)
XLA Modules:
  0.0 81.0 jit_solution(2021808522457435469)
XLA Ops:
  0.7 8.2 %piece_states.3 = (f32[16,1024]{1,0:T(8,128)}, s32[2]{0:T(128)}, bf16[1536,128]{1,0:T(8,128)(2,1)}, bf16[1536,128]{1,0:T(8,128)(2,1)}, bf16[1536,128]{1,0:T(8,12...) custom-call(s32[8]{0:T(128)} %len_ref.11, ...), custom_call_target="tpu_custom_call" | custom-call | flops 1073741824 | bytes 8388608 | tf_op jit(solution)/shard_map/piece_states/pallas_call | solution.py:241
  8.8 3.0 %collective-permute-start = (bf16[528,128]{1,0:T(8,128)(2,1)}, bf16[528,128]{1,0:T(8,128)(2,1)S(1)}, u32[]{:S(2)}, u32[]{:S(2)}) collective-permute-start(bf16[528,128]{1,0:T(8,128)(2,1)} %get-tuple-element.73), channel_id=1, source_target_pairs={{0,2},{2,0},{4,6},{6,4},{8,10},{10,8},{12,14},{14,12},{1,3},{3,1},... | collective-permute-start | bytes 405512 | tf_op jit(solution)/shard_map/ppermute | solution.py:606
  11.9 1.6 %collective-permute-start.1 = (bf16[528,128]{1,0:T(8,128)(2,1)}, bf16[528,128]{1,0:T(8,128)(2,1)S(1)}, u32[]{:S(2)}, u32[]{:S(2)}) collective-permute-start(bf16[528,128]{1,0:T(8,128)(2,1)} %get-tuple-element.74), channel_id=1, source_target_pairs={{0,4},{2,6},{4,0},{6,2},{8,12},{10,14},{12,8},{14,10},{1,5},{3,7},... | collective-permute-start | bytes 405512 | tf_op jit(solution)/shard_map/ppermute | solution.py:606
  13.5 0.0 collective-permute-start.2
  13.5 1.2 %slice.3 = s32[1]{0:T(128)} slice(s32[2]{0:T(128)} %get-tuple-element.80.flag_ref), slice={[1:2]} | slice | bytes 8 | tf_op jit(solution)/shard_map/slice | solution.py:623
  15.4 0.6 reshape.11.gain_ref
  16.0 0.3 conditional.1
  16.0 0.3 broadcast_in_dim.2
  16.3 0.0 copy-start.4
  16.3 0.0 collective-permute-done.refs_1_
  16.4 2.2 %collective-permute-done.1.refs_2_ = bf16[528,128]{1,0:T(8,128)(2,1)S(1)} collective-permute-done((bf16[528,128]{1,0:T(8,128)(2,1)}, bf16[528,128]{1,0:T(8,128)(2,1)S(1)}, u32[]{:S(2)}, u32[]{:S(2)}) %collective-permute-start.1) | collective-permute-done | bytes 135200 | tf_op jit(solution)/shard_map/ppermute | solution.py:606
  18.6 1.3 %collective-permute-done.2.refs_3_ = bf16[528,128]{1,0:T(8,128)(2,1)S(1)} collective-permute-done((bf16[528,128]{1,0:T(8,128)(2,1)}, bf16[528,128]{1,0:T(8,128)(2,1)S(1)}, u32[]{:S(2)}, u32[]{:S(2)}) %collective-permute-start.2) | collective-permute-done | bytes 135200 | tf_op jit(solution)/shard_map/ppermute | solution.py:606
  19.8 0.7 leave_quad.1
  20.6 4.7 %collective-permute-start.3 = (bf16[4,128,128]{2,1,0:T(8,128)(2,1)S(1)}, bf16[4,128,128]{2,1,0:T(8,128)(2,1)S(1)}, u32[]{:S(2)}, u32[]{:S(2)}) collective-permute-start(bf16[4,128,128]{2,1,0:T(8,128)(2,1)S(1)} %leave_quad.1), channel_id=1, source_target_pairs={{0,8},{2,10},{4,12},{6,14},{1,9},{3,11},{5,13},{7,15},{16,24},{18,... | collective-permute-start | bytes 393224 | tf_op jit(solution)/shard_map/ppermute | solution.py:637
  25.2 0.0 copy-start.1
  25.2 1.6 %collective-permute-start.4 = (bf16[1536,128]{1,0:T(8,128)(2,1)}, bf16[1536,128]{1,0:T(8,128)(2,1)S(1)}, u32[]{:S(2)}, u32[]{:S(2)}) collective-permute-start(bf16[1536,128]{1,0:T(8,128)(2,1)} %get-tuple-element.88), channel_id=1, source_target_pairs={{0,2},{2,0},{4,6},{6,4},{8,10},{10,8},{12,14},{14,12},{1,3},{3,1},... | collective-permute-start | bytes 1179656 | tf_op jit(solution)/shard_map/ppermute | solution.py:606
  26.8 1.6 %collective-permute-start.5 = (bf16[1536,128]{1,0:T(8,128)(2,1)S(1)}, bf16[1536,128]{1,0:T(8,128)(2,1)S(1)}, u32[]{:S(2)}, u32[]{:S(2)}) collective-permute-start(bf16[1536,128]{1,0:T(8,128)(2,1)S(1)} %copy-done.13), channel_id=1, source_target_pairs={{0,4},{2,6},{4,0},{6,2},{8,12},{10,14},{12,8},{14,10},{1,5},{3,7},... | collective-permute-start | bytes 1179656 | tf_op jit(solution)/shard_map/ppermute | solution.py:606
  28.4 0.4 collective-permute-start.6
  28.8 14.0 %local_attention.1.local_ref = f32[1024,2048]{1,0:T(8,128)} custom-call(s32[8]{0:T(128)S(1)} %copy-done.9, bf16[1024,2048]{1,0:T(8,128)(2,1)} %q_ref.3, bf16[1024,2048]{1,0:T(8,128)(2,1)} %k_ref.3, bf16[1024,2048]{1,0:T(8,128)(2,1)} %v_ref.3, f32[16,1024]{1,0:T(8,128)} %get-tuple-element.86.crow_ref), custom_call_target="tpu_custom_call" | custom-call | flops 4294967296 | bytes 20971520 | tf_op jit(solution)/shard_map/local_attention/pallas_call | solution.py:355
  42.8 0.0 collective-permute-done.3.refs_4_.refs_9_
  42.8 0.0 collective-permute-done.4.refs_5_
  42.8 0.0 collective-permute-done.5.refs_6_
  42.8 1.9 %collective-permute-done.6.refs_7_ = bf16[1536,128]{1,0:T(8,128)(2,1)S(1)} collective-permute-done((bf16[1536,128]{1,0:T(8,128)(2,1)S(1)}, bf16[1536,128]{1,0:T(8,128)(2,1)S(1)}, u32[]{:S(2)}, u32[]{:S(2)}) %collective-permute-start.6) | collective-permute-done | bytes 393248 | tf_op jit(solution)/shard_map/ppermute | solution.py:606
  44.7 0.8 enter_states.1
  45.5 0.9 %collective-permute-start.7 = (bf16[4,128,128]{2,1,0:T(8,128)(2,1)S(1)}, bf16[4,128,128]{2,1,0:T(8,128)(2,1)S(1)}, u32[]{:S(2)}, u32[]{:S(2)}) collective-permute-start(bf16[4,128,128]{2,1,0:T(8,128)(2,1)S(1)} %get-tuple-element.93), channel_id=1, source_target_pairs={{0,2},{2,0},{4,6},{6,4},{8,10},{10,8},{12,14},{14,12},{1,3},{3,1},... | collective-permute-start | bytes 393224 | tf_op jit(solution)/shard_map/ppermute | solution.py:606
  46.4 3.0 %collective-permute-start.8 = (bf16[4,128,128]{2,1,0:T(8,128)(2,1)S(1)}, bf16[4,128,128]{2,1,0:T(8,128)(2,1)S(1)}, u32[]{:S(2)}, u32[]{:S(2)}) collective-permute-start(bf16[4,128,128]{2,1,0:T(8,128)(2,1)S(1)} %get-tuple-element.94), channel_id=1, source_target_pairs={{0,4},{2,6},{4,0},{6,2},{8,12},{10,14},{12,8},{14,10},{1,5},{3,7},... | collective-permute-start | bytes 393224 | tf_op jit(solution)/shard_map/ppermute | solution.py:606
  49.3 0.0 collective-permute-start.9
  49.3 1.5 %final_states.1 = (bf16[4,128,128]{2,1,0:T(8,128)(2,1)S(1)}, bf16[4,128,128]{2,1,0:T(8,128)(2,1)S(1)}, bf16[4,128,128]{2,1,0:T(8,128)(2,1)S(1)}, bf16[4,128,128]...) custom-call(s32[8]{0:T(128)S(1)} %copy-done.9, ...), custom_call_target="tpu_custom_call" | custom-call | tf_op jit(solution)/shard_map/final_states/pallas_call | solution.py:505
  50.9 0.0 collective-permute-done.7.e1
  50.9 0.0 copy-start.6
  50.9 1.6 %collective-permute-done.8.e2 = bf16[4,128,128]{2,1,0:T(8,128)(2,1)S(1)} collective-permute-done((bf16[4,128,128]{2,1,0:T(8,128)(2,1)S(1)}, bf16[4,128,128]{2,1,0:T(8,128)(2,1)S(1)}, u32[]{:S(2)}, u32[]{:S(2)}) %collective-permute-start.8) | collective-permute-done | bytes 131104 | tf_op jit(solution)/shard_map/ppermute | solution.py:606
  52.4 2.8 %collective-permute-done.9.e3 = bf16[4,128,128]{2,1,0:T(8,128)(2,1)S(1)} collective-permute-done((bf16[4,128,128]{2,1,0:T(8,128)(2,1)S(1)}, bf16[4,128,128]{2,1,0:T(8,128)(2,1)S(1)}, u32[]{:S(2)}, u32[]{:S(2)}) %collective-permute-start.9) | collective-permute-done | bytes 131104 | tf_op jit(solution)/shard_map/ppermute | solution.py:606
  55.2 0.5 collective-permute-start.10
  55.7 1.5 %collective-permute-start.11 = (bf16[4,128,128]{2,1,0:T(8,128)(2,1)S(1)}, bf16[4,128,128]{2,1,0:T(8,128)(2,1)S(1)}, u32[]{:S(2)}, u32[]{:S(2)}) collective-permute-start(bf16[4,128,128]{2,1,0:T(8,128)(2,1)S(1)} %get-tuple-element.117), channel_id=1, source_target_pairs={{0,4},{2,6},{4,0},{6,2},{8,12},{10,14},{12,8},{14,10},{1,5},{3,7},... | collective-permute-start | bytes 393224 | tf_op jit(solution)/shard_map/ppermute | solution.py:606
  57.2 1.5 %collective-permute-start.12 = (bf16[4,128,128]{2,1,0:T(8,128)(2,1)S(1)}, bf16[4,128,128]{2,1,0:T(8,128)(2,1)S(1)}, u32[]{:S(2)}, u32[]{:S(2)}) collective-permute-start(bf16[4,128,128]{2,1,0:T(8,128)(2,1)S(1)} %get-tuple-element.118), channel_id=1, source_target_pairs={{0,6},{2,4},{4,2},{6,0},{8,14},{10,12},{12,10},{14,8},{1,7},{3,5},... | collective-permute-start | bytes 393224 | tf_op jit(solution)/shard_map/ppermute | solution.py:606
  58.7 1.1 %collective-permute-start.13 = (bf16[4,128,128]{2,1,0:T(8,128)(2,1)S(1)}, bf16[4,128,128]{2,1,0:T(8,128)(2,1)S(1)}, u32[]{:S(2)}, u32[]{:S(2)}) collective-permute-start(bf16[4,128,128]{2,1,0:T(8,128)(2,1)S(1)} %get-tuple-element.119), channel_id=1, source_target_pairs={{0,8},{2,10},{4,12},{6,14},{8,0},{10,2},{12,4},{14,6},{1,9},{3,11}... | collective-permute-start | bytes 393224 | tf_op jit(solution)/shard_map/ppermute | solution.py:606
  59.8 1.8 %collective-permute-start.14 = (bf16[4,128,128]{2,1,0:T(8,128)(2,1)S(1)}, bf16[4,128,128]{2,1,0:T(8,128)(2,1)S(1)}, u32[]{:S(2)}, u32[]{:S(2)}) collective-permute-start(bf16[4,128,128]{2,1,0:T(8,128)(2,1)S(1)} %get-tuple-element.120), channel_id=1, source_target_pairs={{0,10},{2,8},{4,14},{6,12},{8,2},{10,0},{12,6},{14,4},{1,11},{3,9}... | collective-permute-start | bytes 393224 | tf_op jit(solution)/shard_map/ppermute | solution.py:606
  61.6 0.0 collective-permute-done.10.refs_1_
  61.6 2.0 %collective-permute-start.15 = (bf16[4,128,128]{2,1,0:T(8,128)(2,1)S(1)}, bf16[4,128,128]{2,1,0:T(8,128)(2,1)S(1)}, u32[]{:S(2)}, u32[]{:S(2)}) collective-permute-start(bf16[4,128,128]{2,1,0:T(8,128)(2,1)S(1)} %get-tuple-element.121), channel_id=1, source_target_pairs={{0,12},{2,14},{4,8},{6,10},{8,4},{10,6},{12,0},{14,2},{1,13},{3,15... | collective-permute-start | bytes 393224 | tf_op jit(solution)/shard_map/ppermute | solution.py:606
  63.6 0.0 collective-permute-done.11.refs_2_
  63.6 2.8 %collective-permute-start.16 = (bf16[4,128,128]{2,1,0:T(8,128)(2,1)S(1)}, bf16[4,128,128]{2,1,0:T(8,128)(2,1)S(1)}, u32[]{:S(2)}, u32[]{:S(2)}) collective-permute-start(bf16[4,128,128]{2,1,0:T(8,128)(2,1)S(1)} %get-tuple-element.122), channel_id=1, source_target_pairs={{0,14},{2,12},{4,10},{6,8},{8,6},{10,4},{12,2},{14,0},{1,15},{3,13... | collective-permute-start | bytes 393224 | tf_op jit(solution)/shard_map/ppermute | solution.py:606
  66.4 13.1 %finish.1 = bf16[1024,2048]{1,0:T(8,128)(2,1)} custom-call(s32[8]{0:T(128)S(1)} %copy-done.9, bf16[1024,2048]{1,0:T(8,128)(2,1)} %q_ref.3, bf16[4,128,128]{2,1,0:T(8,128)(2,1)} %copy-done.2, bf16[4,128,128]{2,1,0:T(8,128)(2,1)} %copy-done.6, bf16[4,128,128]{2,1,0:T(8,128)(2,1)} %copy-done.7, bf16[4,128,128]{2,1,0:T(8,128)(2,1)} %copy-done.8, ...), custom_call_target="tpu_custom_call" | custom-call | flops 536870912 | bytes 20971520 | tf_op jit(solution)/shard_map/finish/pallas_call | solution.py:582
  79.5 0.0 collective-permute-done.12.refs_3_
  79.5 0.0 collective-permute-done.13.refs_4_
  79.5 0.0 collective-permute-done.14.refs_5_
  79.5 0.0 collective-permute-done.15.refs_6_
  79.5 0.0 collective-permute-done.16.refs_7_
  79.5 1.5 %pick_owned.1 = bf16[1,16,128,128]{3,2,1,0:T(8,128)(2,1)} custom-call(s32[2]{0:T(128)S(1)} %copy-done.3, bf16[4,128,128]{2,1,0:T(8,128)(2,1)S(1)} %get-tuple-element.115.refs_0_, bf16[4,128,128]{2,1,0:T(8,128)(2,1)S(1)} %collective-permute-done.10.refs_1_, bf16[4,128,128]{2,1,0:T(8,128)(2,1)S(1)} %collective-permute-done.11.refs_2_, ...), custom_call_target="tpu_custom_call" | custom-call | tf_op jit(solution)/shard_map/pick_owned/pallas_call | solution.py:534
  (25 shorter events, 0.1 us)
Async XLA Ops:
  0.6 14.8 %copy-start.11 = (bf16[2048]{0:T(1024)(128)(2,1)S(1)}, bf16[2048]{0:T(1024)(128)(2,1)}, u32[]{:S(2)}) copy-start(bf16[2048]{0:T(1024)(128)(2,1)} %param.15) | copy-start | bytes 12292
  0.6 15.4 %copy-start.5 = (f32[1024,16]{0,1:T(8,128)S(1)}, f32[1024,16]{0,1:T(8,128)}, u32[]{:S(2)}) copy-start(f32[1024,16]{0,1:T(8,128)} %param.13) | copy-start | bytes 196612
  0.7 15.3 %copy-start.9 = (s32[8]{0:T(128)S(1)}, s32[8]{0:T(128)}, u32[]{:S(2)}) copy-start(s32[8]{0:T(128)} %len_ref.11) | copy-start | bytes 100
  0.7 15.3 %copy-start.10 = (s32[8]{0:T(128)S(1)}, s32[8]{0:T(128)}, u32[]{:S(2)}) copy-start(s32[8]{0:T(128)} %own_ref.3) | copy-start | bytes 100
  8.8 7.5 %collective-permute-start = (bf16[528,128]{1,0:T(8,128)(2,1)}, bf16[528,128]{1,0:T(8,128)(2,1)S(1)}, u32[]{:S(2)}, u32[]{:S(2)}) collective-permute-start(bf16[528,128]{1,0:T(8,128)(2,1)} %get-tuple-element.73), channel_id=1, source_target_pairs={{0,2},{2,0},{4,6},{6,4},{8,10},{10,8},{12,14},{14,12},{1,3},{3,1},... | collective-permute-start | bytes 405512 | tf_op jit(solution)/shard_map/ppermute | solution.py:606
  11.9 6.7 %collective-permute-start.1 = (bf16[528,128]{1,0:T(8,128)(2,1)}, bf16[528,128]{1,0:T(8,128)(2,1)S(1)}, u32[]{:S(2)}, u32[]{:S(2)}) collective-permute-start(bf16[528,128]{1,0:T(8,128)(2,1)} %get-tuple-element.74), channel_id=1, source_target_pairs={{0,4},{2,6},{4,0},{6,2},{8,12},{10,14},{12,8},{14,10},{1,5},{3,7},... | collective-permute-start | bytes 405512 | tf_op jit(solution)/shard_map/ppermute | solution.py:606
  13.5 6.3 %collective-permute-start.2 = (bf16[528,128]{1,0:T(8,128)(2,1)}, bf16[528,128]{1,0:T(8,128)(2,1)S(1)}, u32[]{:S(2)}, u32[]{:S(2)}) collective-permute-start(bf16[528,128]{1,0:T(8,128)(2,1)} %get-tuple-element.75), channel_id=1, source_target_pairs={{0,6},{2,4},{4,2},{6,0},{8,14},{10,12},{12,10},{14,8},{1,7},{3,5},... | collective-permute-start | bytes 405512 | tf_op jit(solution)/shard_map/ppermute | solution.py:606
  16.0 3.8 %copy-start = (bf16[528,128]{1,0:T(8,128)(2,1)S(1)}, bf16[528,128]{1,0:T(8,128)(2,1)}, u32[]{:S(2)}) copy-start(bf16[528,128]{1,0:T(8,128)(2,1)} %get-tuple-element.81.refs_0_) | copy-start | bytes 405508
  16.0 10.8 %copy-start.13 = (bf16[1536,128]{1,0:T(8,128)(2,1)S(1)}, bf16[1536,128]{1,0:T(8,128)(2,1)}, u32[]{:S(2)}) copy-start(bf16[1536,128]{1,0:T(8,128)(2,1)} %get-tuple-element.89) | copy-start | bytes 1179652
  16.0 12.4 %copy-start.12 = (bf16[1536,128]{1,0:T(8,128)(2,1)S(1)}, bf16[1536,128]{1,0:T(8,128)(2,1)}, u32[]{:S(2)}) copy-start(bf16[1536,128]{1,0:T(8,128)(2,1)} %get-tuple-element.90) | copy-start | bytes 1179652
  16.3 3.5 %copy-start.4 = (bf16[4,2048,128]{2,1,0:T(8,128)(2,1)}, bf16[4,2048,128]{2,1,0:T(8,128)(2,1)S(1)}, u32[]{:S(2)}) copy-start(bf16[4,2048,128]{2,1,0:T(8,128)(2,1)S(1)} %get-tuple-element.123.refs_8_) | copy-start | bytes 6291460
  20.6 22.2 %collective-permute-start.3 = (bf16[4,128,128]{2,1,0:T(8,128)(2,1)S(1)}, bf16[4,128,128]{2,1,0:T(8,128)(2,1)S(1)}, u32[]{:S(2)}, u32[]{:S(2)}) collective-permute-start(bf16[4,128,128]{2,1,0:T(8,128)(2,1)S(1)} %leave_quad.1), channel_id=1, source_target_pairs={{0,8},{2,10},{4,12},{6,14},{1,9},{3,11},{5,13},{7,15},{16,24},{18,... | collective-permute-start | bytes 393224 | tf_op jit(solution)/shard_map/ppermute | solution.py:637
  25.2 24.1 %copy-start.1 = (bf16[1536,128]{1,0:T(8,128)(2,1)S(1)}, bf16[1536,128]{1,0:T(8,128)(2,1)}, u32[]{:S(2)}) copy-start(bf16[1536,128]{1,0:T(8,128)(2,1)} %get-tuple-element.96.refs_4_) | copy-start | bytes 1179652
  25.2 17.5 %collective-permute-start.4 = (bf16[1536,128]{1,0:T(8,128)(2,1)}, bf16[1536,128]{1,0:T(8,128)(2,1)S(1)}, u32[]{:S(2)}, u32[]{:S(2)}) collective-permute-start(bf16[1536,128]{1,0:T(8,128)(2,1)} %get-tuple-element.88), channel_id=1, source_target_pairs={{0,2},{2,0},{4,6},{6,4},{8,10},{10,8},{12,14},{14,12},{1,3},{3,1},... | collective-permute-start | bytes 1179656 | tf_op jit(solution)/shard_map/ppermute | solution.py:606
  26.8 15.9 %collective-permute-start.5 = (bf16[1536,128]{1,0:T(8,128)(2,1)S(1)}, bf16[1536,128]{1,0:T(8,128)(2,1)S(1)}, u32[]{:S(2)}, u32[]{:S(2)}) collective-permute-start(bf16[1536,128]{1,0:T(8,128)(2,1)S(1)} %copy-done.13), channel_id=1, source_target_pairs={{0,4},{2,6},{4,0},{6,2},{8,12},{10,14},{12,8},{14,10},{1,5},{3,7},... | collective-permute-start | bytes 1179656 | tf_op jit(solution)/shard_map/ppermute | solution.py:606
  28.4 16.3 %collective-permute-start.6 = (bf16[1536,128]{1,0:T(8,128)(2,1)S(1)}, bf16[1536,128]{1,0:T(8,128)(2,1)S(1)}, u32[]{:S(2)}, u32[]{:S(2)}) collective-permute-start(bf16[1536,128]{1,0:T(8,128)(2,1)S(1)} %copy-done.12), channel_id=1, source_target_pairs={{0,6},{2,4},{4,2},{6,0},{8,14},{10,12},{12,10},{14,8},{1,7},{3,5},... | collective-permute-start | bytes 1179656 | tf_op jit(solution)/shard_map/ppermute | solution.py:606
  45.4 5.4 %copy-start.2 = (bf16[4,128,128]{2,1,0:T(8,128)(2,1)}, bf16[4,128,128]{2,1,0:T(8,128)(2,1)S(1)}, u32[]{:S(2)}) copy-start(bf16[4,128,128]{2,1,0:T(8,128)(2,1)S(1)} %get-tuple-element.109.e0) | copy-start | bytes 393220
  45.5 5.4 %collective-permute-start.7 = (bf16[4,128,128]{2,1,0:T(8,128)(2,1)S(1)}, bf16[4,128,128]{2,1,0:T(8,128)(2,1)S(1)}, u32[]{:S(2)}, u32[]{:S(2)}) collective-permute-start(bf16[4,128,128]{2,1,0:T(8,128)(2,1)S(1)} %get-tuple-element.93), channel_id=1, source_target_pairs={{0,2},{2,0},{4,6},{6,4},{8,10},{10,8},{12,14},{14,12},{1,3},{3,1},... | collective-permute-start | bytes 393224 | tf_op jit(solution)/shard_map/ppermute | solution.py:606
  46.4 6.1 %collective-permute-start.8 = (bf16[4,128,128]{2,1,0:T(8,128)(2,1)S(1)}, bf16[4,128,128]{2,1,0:T(8,128)(2,1)S(1)}, u32[]{:S(2)}, u32[]{:S(2)}) collective-permute-start(bf16[4,128,128]{2,1,0:T(8,128)(2,1)S(1)} %get-tuple-element.94), channel_id=1, source_target_pairs={{0,4},{2,6},{4,0},{6,2},{8,12},{10,14},{12,8},{14,10},{1,5},{3,7},... | collective-permute-start | bytes 393224 | tf_op jit(solution)/shard_map/ppermute | solution.py:606
  49.3 5.9 %collective-permute-start.9 = (bf16[4,128,128]{2,1,0:T(8,128)(2,1)S(1)}, bf16[4,128,128]{2,1,0:T(8,128)(2,1)S(1)}, u32[]{:S(2)}, u32[]{:S(2)}) collective-permute-start(bf16[4,128,128]{2,1,0:T(8,128)(2,1)S(1)} %get-tuple-element.95), channel_id=1, source_target_pairs={{0,6},{2,4},{4,2},{6,0},{8,14},{10,12},{12,10},{14,8},{1,7},{3,5},... | collective-permute-start | bytes 393224 | tf_op jit(solution)/shard_map/ppermute | solution.py:606
  50.9 15.5 %copy-start.6 = (bf16[4,128,128]{2,1,0:T(8,128)(2,1)}, bf16[4,128,128]{2,1,0:T(8,128)(2,1)S(1)}, u32[]{:S(2)}) copy-start(bf16[4,128,128]{2,1,0:T(8,128)(2,1)S(1)} %collective-permute-done.7.e1) | copy-start | bytes 393220
  52.4 13.9 %copy-start.7 = (bf16[4,128,128]{2,1,0:T(8,128)(2,1)}, bf16[4,128,128]{2,1,0:T(8,128)(2,1)S(1)}, u32[]{:S(2)}) copy-start(bf16[4,128,128]{2,1,0:T(8,128)(2,1)S(1)} %collective-permute-done.8.e2) | copy-start | bytes 393220
  55.2 11.2 %copy-start.8 = (bf16[4,128,128]{2,1,0:T(8,128)(2,1)}, bf16[4,128,128]{2,1,0:T(8,128)(2,1)S(1)}, u32[]{:S(2)}) copy-start(bf16[4,128,128]{2,1,0:T(8,128)(2,1)S(1)} %collective-permute-done.9.e3) | copy-start | bytes 393220
  55.2 24.3 %copy-start.3 = (s32[2]{0:T(128)S(1)}, s32[2]{0:T(128)}, u32[]{:S(2)}) copy-start(s32[2]{0:T(128)} %get-tuple-element.80.flag_ref) | copy-start | bytes 28
  55.2 6.4 %collective-permute-start.10 = (bf16[4,128,128]{2,1,0:T(8,128)(2,1)S(1)}, bf16[4,128,128]{2,1,0:T(8,128)(2,1)S(1)}, u32[]{:S(2)}, u32[]{:S(2)}) collective-permute-start(bf16[4,128,128]{2,1,0:T(8,128)(2,1)S(1)} %get-tuple-element.116), channel_id=1, source_target_pairs={{0,2},{2,0},{4,6},{6,4},{8,10},{10,8},{12,14},{14,12},{1,3},{3,1},... | collective-permute-start | bytes 393224 | tf_op jit(solution)/shard_map/ppermute | solution.py:606
  55.7 7.8 %collective-permute-start.11 = (bf16[4,128,128]{2,1,0:T(8,128)(2,1)S(1)}, bf16[4,128,128]{2,1,0:T(8,128)(2,1)S(1)}, u32[]{:S(2)}, u32[]{:S(2)}) collective-permute-start(bf16[4,128,128]{2,1,0:T(8,128)(2,1)S(1)} %get-tuple-element.117), channel_id=1, source_target_pairs={{0,4},{2,6},{4,0},{6,2},{8,12},{10,14},{12,8},{14,10},{1,5},{3,7},... | collective-permute-start | bytes 393224 | tf_op jit(solution)/shard_map/ppermute | solution.py:606
  57.2 22.2 %collective-permute-start.12 = (bf16[4,128,128]{2,1,0:T(8,128)(2,1)S(1)}, bf16[4,128,128]{2,1,0:T(8,128)(2,1)S(1)}, u32[]{:S(2)}, u32[]{:S(2)}) collective-permute-start(bf16[4,128,128]{2,1,0:T(8,128)(2,1)S(1)} %get-tuple-element.118), channel_id=1, source_target_pairs={{0,6},{2,4},{4,2},{6,0},{8,14},{10,12},{12,10},{14,8},{1,7},{3,5},... | collective-permute-start | bytes 393224 | tf_op jit(solution)/shard_map/ppermute | solution.py:606
  58.7 20.8 %collective-permute-start.13 = (bf16[4,128,128]{2,1,0:T(8,128)(2,1)S(1)}, bf16[4,128,128]{2,1,0:T(8,128)(2,1)S(1)}, u32[]{:S(2)}, u32[]{:S(2)}) collective-permute-start(bf16[4,128,128]{2,1,0:T(8,128)(2,1)S(1)} %get-tuple-element.119), channel_id=1, source_target_pairs={{0,8},{2,10},{4,12},{6,14},{8,0},{10,2},{12,4},{14,6},{1,9},{3,11}... | collective-permute-start | bytes 393224 | tf_op jit(solution)/shard_map/ppermute | solution.py:606
  59.8 19.7 %collective-permute-start.14 = (bf16[4,128,128]{2,1,0:T(8,128)(2,1)S(1)}, bf16[4,128,128]{2,1,0:T(8,128)(2,1)S(1)}, u32[]{:S(2)}, u32[]{:S(2)}) collective-permute-start(bf16[4,128,128]{2,1,0:T(8,128)(2,1)S(1)} %get-tuple-element.120), channel_id=1, source_target_pairs={{0,10},{2,8},{4,14},{6,12},{8,2},{10,0},{12,6},{14,4},{1,11},{3,9}... | collective-permute-start | bytes 393224 | tf_op jit(solution)/shard_map/ppermute | solution.py:606
  61.6 17.9 %collective-permute-start.15 = (bf16[4,128,128]{2,1,0:T(8,128)(2,1)S(1)}, bf16[4,128,128]{2,1,0:T(8,128)(2,1)S(1)}, u32[]{:S(2)}, u32[]{:S(2)}) collective-permute-start(bf16[4,128,128]{2,1,0:T(8,128)(2,1)S(1)} %get-tuple-element.121), channel_id=1, source_target_pairs={{0,12},{2,14},{4,8},{6,10},{8,4},{10,6},{12,0},{14,2},{1,13},{3,15... | collective-permute-start | bytes 393224 | tf_op jit(solution)/shard_map/ppermute | solution.py:606
  63.6 15.9 %collective-permute-start.16 = (bf16[4,128,128]{2,1,0:T(8,128)(2,1)S(1)}, bf16[4,128,128]{2,1,0:T(8,128)(2,1)S(1)}, u32[]{:S(2)}, u32[]{:S(2)}) collective-permute-start(bf16[4,128,128]{2,1,0:T(8,128)(2,1)S(1)} %get-tuple-element.122), channel_id=1, source_target_pairs={{0,14},{2,12},{4,10},{6,8},{8,6},{10,4},{12,2},{14,0},{1,15},{3,13... | collective-permute-start | bytes 393224 | tf_op jit(solution)/shard_map/ppermute | solution.py:606

commit v2 on v1

--- a/solution.py
+++ b/solution.py
@@ -419,30 +419,24 @@
 
 
 def enter_kernel(rows, len_ref, *refs):
-    in_ref, out_refs, last_ref, state_ref = refs[MEMBERS], refs[MEMBERS + 1 : -2], refs[-2], refs[-1]
+    in_ref, out_ref, last_ref = refs[MEMBERS:]
     gather_last(refs[:MEMBERS], last_ref)
     hp = in_ref.shape[0]
 
     def note(i, e, state):
-        state_ref[e, i] = state
+        out_ref[e, i] = state.astype(BF16)
 
     for i in range(hp):
         scan_quad(rows, len_ref, last_ref, in_ref[i].astype(F32), i, hp, functools.partial(note, i))
-    me = lax.axis_index("seq") % MEMBERS
-    for x, out_ref in enumerate(out_refs):
-        out_ref[...] = state_ref[me ^ x].astype(BF16)
 
 
 def enter_states(doc_lengths, last, coming, rows):
     return pl.pallas_call(
         functools.partial(enter_kernel, rows),
         in_specs=[SMEM] + [VMEM] * (MEMBERS + 1),
-        out_specs=[VMEM] * MEMBERS,
-        out_shape=[jax.ShapeDtypeStruct(coming.shape, BF16)] * MEMBERS,
-        scratch_shapes=[
-            pltpu.VMEM((MEMBERS,) + last[0].shape, BF16),
-            pltpu.VMEM((MEMBERS,) + coming.shape, F32),
-        ],
+        out_specs=VMEM,
+        out_shape=jax.ShapeDtypeStruct((MEMBERS,) + coming.shape, BF16),
+        scratch_shapes=[pltpu.VMEM((MEMBERS,) + last[0].shape, BF16)],
         compiler_params=SMALL,
         name="enter_states",
     )(doc_lengths, *last, coming)
@@ -541,30 +535,20 @@
     )(flags, *arrived)
 
 
-def finish_kernel(len_ref, q_ref, e0, e1, e2, e3, local_ref, gate_ref, gain_ref, crow_ref, out_ref, ccol_ref):
+def finish_kernel(len_ref, q_ref, enter_ref, local_ref, gate_ref, gain_ref, crow_ref, out_ref, ccol_ref):
     rows = q_ref.shape[0]
     step = pl.program_id(0)
-    me = lax.axis_index("seq")
-    hp = e0.shape[0]
+    first = lax.axis_index("seq") * rows
 
     @pl.when(step == 0)
     def _():
         fill_columns(crow_ref, ccol_ref)
 
-    def entering(h):
-        far = (h // hp) ^ (me % MEMBERS)
-        state = e0[h % hp]
-        for x, ref in ((1, e1), (2, e2), (3, e3)):
-            state = jnp.where(far == x, ref[h % hp], state)
-        return state
-
-    first = me * rows
     reach = run_end(read_ends(len_ref, len_ref.shape[0]), first - 1) - first
     cols = [head_column(ccol_ref, step * 2 + i) for i in range(2)]
-    states = [entering(step * 2 + i) for i in range(2)]
     for t0 in range(0, rows, 256):
         span = slice(t0, t0 + 256)
-        carry = [dot(q_ref[span, i * 128 : (i + 1) * 128], states[i]) for i in range(2)]
+        carry = [dot(q_ref[span, i * 128 : (i + 1) * 128], enter_ref[i]) for i in range(2)]
         inside = t0 + iota((256, 1), 0) < reach
         for i in range(2):
             lanes = slice(i * 128, (i + 1) * 128)
@@ -582,9 +566,15 @@
     return pl.pallas_call(
         finish_kernel,
         grid=(heads // 2,),
-        in_specs=[SMEM, wide]
-        + [whole(e.shape) for e in entering]
-        + [wide, wide, pl.BlockSpec((1, 256), lambda j: (0, j)), whole((heads, rows))],
+        in_specs=[
+            SMEM,
+            wide,
+            pl.BlockSpec((2, 128, 128), lambda j: (j, 0, 0)),
+            wide,
+            wide,
+            pl.BlockSpec((1, 256), lambda j: (0, j)),
+            whole((heads, rows)),
+        ],
         out_specs=wide,
         out_shape=jax.ShapeDtypeStruct((rows, heads * 128), BF16),
         scratch_shapes=[pltpu.VMEM((rows, 128), F32)],
@@ -593,7 +583,7 @@
             flops=heads * rows * 128 * 256, bytes_accessed=rows * heads * 128 * 10, transcendentals=heads * rows * 256
         ),
         name="finish",
-    )(doc_lengths, queries, *entering, local, gate, gain, crow)
+    )(doc_lengths, queries, entering, local, gate, gain, crow)
 
 
 def swap(x, groups=None):
@@ -639,9 +629,8 @@
     local = local_attention(doc_lengths, queries, keys, values, crow_1)
     coming, local, side = barrier((coming[0], local, side))
 
-    entering = by_distance(enter_states(doc_lengths, last, coming, rows), spread)
+    entering = swap(enter_states(doc_lengths, last, coming, rows), near).reshape(heads, 128, 128)
     finals = final_states(doc_lengths, owner_ids, last, side, rest, coming, rows, spread)
-    entering, finals = barrier((entering, finals))
     arrived = by_distance(finals, spread)
     mixed = finish(doc_lengths, queries, entering, local, gate, gain, crow)
     return mixed, pick_owned(flags, arrived, heads)

time: 81.6 us -> 95.8 us (1.17)
  waiting for transfers between devices: 9.71 us -> 23.5 us
  starting transfers between devices: 27.9 us -> 26.9 us
    ppermute x16 -> x13, waiting for transfers between devices: 9.71 us -> 23.5 us  [by_distance(): lax.ppermute(parcels[x], 'seq', [(s, s ^ x) for s in range(spread)])]
    ppermute x16 -> x13, starting transfers between devices: 23.2 us -> 17.9 us  [by_distance(): lax.ppermute(parcels[x], 'seq', [(s, s ^ x) for s in range(spread)])]
    all_to_all x0 -> x1, starting transfers between devices: none -> 4.31 us  [swap(): lax.all_to_all(x, 'seq', split_axis=0, concat_axis=0, axis_index_groups=g...]
  transfers between devices with their start and end apart: 17 -> 15, of which waited for: 5 -> 7; matrix products, arithmetic and copies ran while one was open for 3% -> 2% of each run, Pallas kernels for 35% -> 18%
where the time goes in v2:
time: 95.8 us; the launch traced here: 95.2 us
  Pallas kernels  40.2 us (42%)
  starting transfers between devices  26.9 us (28%)
  waiting for transfers between devices  23.5 us (25%)
  local copies, waits for them, and re-layouts  3.05 us (3%)
  between operations  1.45 us (2%)
    ppermute x13, waiting for transfers between devices, by_distance(): lax.ppermute(parcels[x], 'seq', [(s, s ^ x) for s in range(spread)])  23.5 us
    ppermute x13, starting transfers between devices, by_distance(): lax.ppermute(parcels[x], 'seq', [(s, s ^ x) for s in range(spread)])  17.9 us
    pallas_call x1, Pallas kernels, local_attention(): pl.pallas_call(local_kernel, grid=(heads // 2,), in_specs=[SMEM, wide, wi...  13.9 us
    pallas_call x1, Pallas kernels, finish(): pl.pallas_call(finish_kernel, grid=(heads // 2,), in_specs=[SMEM, wide, p...  12.9 us
    pallas_call x1, Pallas kernels, piece_states(): pl.pallas_call(functools.partial(pieces_kernel, rest), grid=(MEMBERS,), i...  8.19 us
    ppermute x1, starting transfers between devices, on_device(): coming = [lax.ppermute(leaving, 'seq', onward)]  4.65 us
    all_to_all x1, starting transfers between devices, swap(): lax.all_to_all(x, 'seq', split_axis=0, concat_axis=0, axis_index_groups=g...  4.31 us
  transfers between devices with their start and end apart: 15, of which 7 were waited for; matrix products, arithmetic and copies ran while one was open for 2% of the time, Pallas kernels for 18%

profile of v2, /device:TPU:0, one launch (start us, length us, event | category | flops | bytes accessed | tf_op | source)
XLA Modules:
  0.0 95.2 jit_solution(708653641506177729)
XLA Ops:
  0.6 0.0 copy-start.8
  0.6 0.0 copy-start.5
  0.7 0.0 copy-start.6
  0.7 0.0 copy-start.7
  0.7 8.2 %piece_states.3 = (f32[16,1024]{1,0:T(8,128)}, s32[2]{0:T(128)}, bf16[1536,128]{1,0:T(8,128)(2,1)}, bf16[1536,128]{1,0:T(8,128)(2,1)}, bf16[1536,128]{1,0:T(8,12...) custom-call(s32[8]{0:T(128)} %len_ref.11, ...), custom_call_target="tpu_custom_call" | custom-call | flops 1073741824 | bytes 8388608 | tf_op jit(solution)/shard_map/piece_states/pallas_call | solution.py:241
  8.9 3.0 %collective-permute-start = (bf16[528,128]{1,0:T(8,128)(2,1)}, bf16[528,128]{1,0:T(8,128)(2,1)S(1)}, u32[]{:S(2)}, u32[]{:S(2)}) collective-permute-start(bf16[528,128]{1,0:T(8,128)(2,1)} %get-tuple-element.57), channel_id=1, source_target_pairs={{0,2},{2,0},{4,6},{6,4},{8,10},{10,8},{12,14},{14,12},{1,3},{3,1},... | collective-permute-start | bytes 405512 | tf_op jit(solution)/shard_map/ppermute | solution.py:596
  11.9 1.6 %collective-permute-start.1 = (bf16[528,128]{1,0:T(8,128)(2,1)}, bf16[528,128]{1,0:T(8,128)(2,1)S(1)}, u32[]{:S(2)}, u32[]{:S(2)}) collective-permute-start(bf16[528,128]{1,0:T(8,128)(2,1)} %get-tuple-element.58), channel_id=1, source_target_pairs={{0,4},{2,6},{4,0},{6,2},{8,12},{10,14},{12,8},{14,10},{1,5},{3,7},... | collective-permute-start | bytes 405512 | tf_op jit(solution)/shard_map/ppermute | solution.py:596
  13.5 0.0 collective-permute-start.2
  13.5 1.3 %slice.3 = s32[1]{0:T(128)} slice(s32[2]{0:T(128)} %get-tuple-element.64.flag_ref), slice={[1:2]} | slice | bytes 8 | tf_op jit(solution)/shard_map/slice | solution.py:613
  15.4 0.6 reshape.14.gain_ref
  16.0 0.3 conditional.1
  16.0 0.3 broadcast_in_dim.2
  16.3 0.0 copy-start.3
  16.3 0.0 collective-permute-done.refs_1_
  16.4 2.2 %collective-permute-done.1.refs_2_ = bf16[528,128]{1,0:T(8,128)(2,1)S(1)} collective-permute-done((bf16[528,128]{1,0:T(8,128)(2,1)}, bf16[528,128]{1,0:T(8,128)(2,1)S(1)}, u32[]{:S(2)}, u32[]{:S(2)}) %collective-permute-start.1) | collective-permute-done | bytes 135200 | tf_op jit(solution)/shard_map/ppermute | solution.py:596
  18.6 1.2 %collective-permute-done.2.refs_3_ = bf16[528,128]{1,0:T(8,128)(2,1)S(1)} collective-permute-done((bf16[528,128]{1,0:T(8,128)(2,1)}, bf16[528,128]{1,0:T(8,128)(2,1)S(1)}, u32[]{:S(2)}, u32[]{:S(2)}) %collective-permute-start.2) | collective-permute-done | bytes 135200 | tf_op jit(solution)/shard_map/ppermute | solution.py:596
  19.9 0.7 leave_quad.1
  20.6 4.6 %collective-permute-start.3 = (bf16[4,128,128]{2,1,0:T(8,128)(2,1)S(1)}, bf16[4,128,128]{2,1,0:T(8,128)(2,1)S(1)}, u32[]{:S(2)}, u32[]{:S(2)}) collective-permute-start(bf16[4,128,128]{2,1,0:T(8,128)(2,1)S(1)} %leave_quad.1), channel_id=1, source_target_pairs={{0,8},{2,10},{4,12},{6,14},{1,9},{3,11},{5,13},{7,15},{16,24},{18,... | collective-permute-start | bytes 393224 | tf_op jit(solution)/shard_map/ppermute | solution.py:627
  25.2 0.0 copy-start.1
  25.2 1.6 %collective-permute-start.4 = (bf16[1536,128]{1,0:T(8,128)(2,1)}, bf16[1536,128]{1,0:T(8,128)(2,1)S(1)}, u32[]{:S(2)}, u32[]{:S(2)}) collective-permute-start(bf16[1536,128]{1,0:T(8,128)(2,1)} %get-tuple-element.72), channel_id=1, source_target_pairs={{0,2},{2,0},{4,6},{6,4},{8,10},{10,8},{12,14},{14,12},{1,3},{3,1},... | collective-permute-start | bytes 1179656 | tf_op jit(solution)/shard_map/ppermute | solution.py:596
  26.8 1.6 %collective-permute-start.5 = (bf16[1536,128]{1,0:T(8,128)(2,1)}, bf16[1536,128]{1,0:T(8,128)(2,1)S(1)}, u32[]{:S(2)}, u32[]{:S(2)}) collective-permute-start(bf16[1536,128]{1,0:T(8,128)(2,1)} %get-tuple-element.73), channel_id=1, source_target_pairs={{0,4},{2,6},{4,0},{6,2},{8,12},{10,14},{12,8},{14,10},{1,5},{3,7},... | collective-permute-start | bytes 1179656 | tf_op jit(solution)/shard_map/ppermute | solution.py:596
  28.4 0.4 collective-permute-start.6
  28.8 13.9 %local_attention.1.local_ref = f32[1024,2048]{1,0:T(8,128)} custom-call(s32[8]{0:T(128)S(1)} %copy-done.6, bf16[1024,2048]{1,0:T(8,128)(2,1)} %q_ref.3, bf16[1024,2048]{1,0:T(8,128)(2,1)} %k_ref.3, bf16[1024,2048]{1,0:T(8,128)(2,1)} %v_ref.3, f32[16,1024]{1,0:T(8,128)} %get-tuple-element.70.crow_ref), custom_call_target="tpu_custom_call" | custom-call | flops 4294967296 | bytes 20971520 | tf_op jit(solution)/shard_map/local_attention/pallas_call | solution.py:355
  42.7 0.0 collective-permute-done.3.refs_4_.refs_9_
  42.7 0.0 collective-permute-done.4.refs_5_
  42.7 0.0 collective-permute-done.5.refs_6_
  42.8 2.1 %collective-permute-done.6.refs_7_ = bf16[1536,128]{1,0:T(8,128)(2,1)S(1)} collective-permute-done((bf16[1536,128]{1,0:T(8,128)(2,1)S(1)}, bf16[1536,128]{1,0:T(8,128)(2,1)S(1)}, u32[]{:S(2)}, u32[]{:S(2)}) %collective-permute-start.6) | collective-permute-done | bytes 393248 | tf_op jit(solution)/shard_map/ppermute | solution.py:596
  44.9 1.6 %enter_states.1 = bf16[4,4,128,128]{3,2,1,0:T(8,128)(2,1)} custom-call(s32[8]{0:T(128)S(1)} %copy-done.6, bf16[528,128]{1,0:T(8,128)(2,1)S(1)} %copy-done, bf16[528,128]{1,0:T(8,128)(2,1)S(1)} %collective-permute-done.refs_1_, bf16[528,128]{1,0:T(8,128)(2,1)S(1)} %collective-permute-done.1.refs_2_, bf16[528,128]{1,0:T(8,128)(2,1)S(1)} %collective-permute-done.2.refs_3_, ...), custom_call_target="tpu_custom_call" | custom-call | tf_op jit(solution)/shard_map/enter_states/pallas_call | solution.py:434
  46.5 4.3 %all-to-all-start.1 = ((bf16[4,4,128,128]{3,2,1,0:T(8,128)(2,1)}), bf16[4,4,128,128]{3,2,1,0:T(8,128)(2,1)S(1)}, u32[]{:S(2)}, u32[]{:S(2)}) async-start(bf16[4,4,128,128]{3,2,1,0:T(8,128)(2,1)} %enter_states.1), calls=%async_computation.1 | async-start | bytes 1048576 | tf_op jit(solution)/shard_map/all_to_all | solution.py:590
  50.8 1.4 %final_states.1 = (bf16[4,128,128]{2,1,0:T(8,128)(2,1)S(1)}, bf16[4,128,128]{2,1,0:T(8,128)(2,1)S(1)}, bf16[4,128,128]{2,1,0:T(8,128)(2,1)S(1)}, bf16[4,128,128]...) custom-call(s32[8]{0:T(128)S(1)} %copy-done.6, ...), custom_call_target="tpu_custom_call" | custom-call | tf_op jit(solution)/shard_map/final_states/pallas_call | solution.py:499
  52.2 1.5 %collective-permute-start.10 = (bf16[4,128,128]{2,1,0:T(8,128)(2,1)S(1)}, bf16[4,128,128]{2,1,0:T(8,128)(2,1)S(1)}, u32[]{:S(2)}, u32[]{:S(2)}) collective-permute-start(bf16[4,128,128]{2,1,0:T(8,128)(2,1)S(1)} %get-tuple-element.87), channel_id=1, source_target_pairs={{0,8},{2,10},{4,12},{6,14},{8,0},{10,2},{12,4},{14,6},{1,9},{3,11}... | collective-permute-start | bytes 393224 | tf_op jit(solution)/shard_map/ppermute | solution.py:596
  53.7 2.9 %collective-permute-start.11 = (bf16[4,128,128]{2,1,0:T(8,128)(2,1)S(1)}, bf16[4,128,128]{2,1,0:T(8,128)(2,1)S(1)}, u32[]{:S(2)}, u32[]{:S(2)}) collective-permute-start(bf16[4,128,128]{2,1,0:T(8,128)(2,1)S(1)} %get-tuple-element.88), channel_id=1, source_target_pairs={{0,10},{2,8},{4,14},{6,12},{8,2},{10,0},{12,6},{14,4},{1,11},{3,9}... | collective-permute-start | bytes 393224 | tf_op jit(solution)/shard_map/ppermute | solution.py:596
  56.6 2.4 %collective-permute-start.12 = (bf16[4,128,128]{2,1,0:T(8,128)(2,1)S(1)}, bf16[4,128,128]{2,1,0:T(8,128)(2,1)S(1)}, u32[]{:S(2)}, u32[]{:S(2)}) collective-permute-start(bf16[4,128,128]{2,1,0:T(8,128)(2,1)S(1)} %get-tuple-element.89), channel_id=1, source_target_pairs={{0,12},{2,14},{4,8},{6,10},{8,4},{10,6},{12,0},{14,2},{1,13},{3,15... | collective-permute-start | bytes 393224 | tf_op jit(solution)/shard_map/ppermute | solution.py:596
  59.0 0.9 collective-permute-start.13
  59.9 2.0 %collective-permute-start.7 = (bf16[4,128,128]{2,1,0:T(8,128)(2,1)S(1)}, bf16[4,128,128]{2,1,0:T(8,128)(2,1)S(1)}, u32[]{:S(2)}, u32[]{:S(2)}) collective-permute-start(bf16[4,128,128]{2,1,0:T(8,128)(2,1)S(1)} %get-tuple-element.84), channel_id=1, source_target_pairs={{0,2},{2,0},{4,6},{6,4},{8,10},{10,8},{12,14},{14,12},{1,3},{3,1},... | collective-permute-start | bytes 393224 | tf_op jit(solution)/shard_map/ppermute | solution.py:596
  61.9 5.7 %collective-permute-done.10.refs_4_ = bf16[4,128,128]{2,1,0:T(8,128)(2,1)S(1)} collective-permute-done((bf16[4,128,128]{2,1,0:T(8,128)(2,1)S(1)}, bf16[4,128,128]{2,1,0:T(8,128)(2,1)S(1)}, u32[]{:S(2)}, u32[]{:S(2)}) %collective-permute-start.10) | collective-permute-done | bytes 131104 | tf_op jit(solution)/shard_map/ppermute | solution.py:596
  67.7 0.0 collective-permute-start.8
  67.7 6.3 %collective-permute-done.11.refs_5_ = bf16[4,128,128]{2,1,0:T(8,128)(2,1)S(1)} collective-permute-done((bf16[4,128,128]{2,1,0:T(8,128)(2,1)S(1)}, bf16[4,128,128]{2,1,0:T(8,128)(2,1)S(1)}, u32[]{:S(2)}, u32[]{:S(2)}) %collective-permute-start.11) | collective-permute-done | bytes 131104 | tf_op jit(solution)/shard_map/ppermute | solution.py:596
  74.0 0.0 collective-permute-start.9
  74.0 0.0 collective-permute-done.12.refs_6_
  74.0 0.0 collective-permute-done.13.refs_7_
  74.0 0.0 collective-permute-done.7.refs_1_
  74.0 0.5 collective-permute-done.8.refs_2_
  74.5 5.3 %collective-permute-done.9.refs_3_ = bf16[4,128,128]{2,1,0:T(8,128)(2,1)S(1)} collective-permute-done((bf16[4,128,128]{2,1,0:T(8,128)(2,1)S(1)}, bf16[4,128,128]{2,1,0:T(8,128)(2,1)S(1)}, u32[]{:S(2)}, u32[]{:S(2)}) %collective-permute-start.9) | collective-permute-done | bytes 131104 | tf_op jit(solution)/shard_map/ppermute | solution.py:596
  79.9 1.5 %pick_owned.1 = bf16[1,16,128,128]{3,2,1,0:T(8,128)(2,1)} custom-call(s32[2]{0:T(128)S(1)} %copy-done.2, bf16[4,128,128]{2,1,0:T(8,128)(2,1)S(1)} %get-tuple-element.83.refs_0_, bf16[4,128,128]{2,1,0:T(8,128)(2,1)S(1)} %collective-permute-done.7.refs_1_, bf16[4,128,128]{2,1,0:T(8,128)(2,1)S(1)} %collective-permute-done.8.refs_2_, ...), custom_call_target="tpu_custom_call" | custom-call | tf_op jit(solution)/shard_map/pick_owned/pallas_call | solution.py:528
  81.3 0.0 all-to-all-done.1
  81.4 0.9 copy-done.4
  82.2 12.9 %finish.1 = bf16[1024,2048]{1,0:T(8,128)(2,1)} custom-call(s32[8]{0:T(128)S(1)} %copy-done.6, bf16[1024,2048]{1,0:T(8,128)(2,1)} %q_ref.3, bf16[16,128,128]{2,1,0:T(8,128)(2,1)} %bitcast.3, f32[1024,2048]{1,0:T(8,128)} %local_attention.1.local_ref, bf16[1024,2048]{1,0:T(8,128)(2,1)} %gate_ref.1, bf16[1,2048]{1,0:T(2,128)(2,1)} %reshape.14.gain_ref, ...), custom_call_target="tpu_custom_call" | custom-call | flops 536870912 | bytes 20971520 | tf_op jit(solution)/shard_map/finish/pallas_call | solution.py:566
  (13 shorter events, 0.0 us)
Async XLA Ops:
  0.6 14.8 %copy-start.8 = (bf16[2048]{0:T(1024)(128)(2,1)S(1)}, bf16[2048]{0:T(1024)(128)(2,1)}, u32[]{:S(2)}) copy-start(bf16[2048]{0:T(1024)(128)(2,1)} %param.15) | copy-start | bytes 12292
  0.6 15.4 %copy-start.5 = (f32[1024,16]{0,1:T(8,128)S(1)}, f32[1024,16]{0,1:T(8,128)}, u32[]{:S(2)}) copy-start(f32[1024,16]{0,1:T(8,128)} %param.13) | copy-start | bytes 196612
  0.7 15.4 %copy-start.6 = (s32[8]{0:T(128)S(1)}, s32[8]{0:T(128)}, u32[]{:S(2)}) copy-start(s32[8]{0:T(128)} %len_ref.11) | copy-start | bytes 100
  0.7 15.4 %copy-start.7 = (s32[8]{0:T(128)S(1)}, s32[8]{0:T(128)}, u32[]{:S(2)}) copy-start(s32[8]{0:T(128)} %own_ref.3) | copy-start | bytes 100
  8.9 7.5 %collective-permute-start = (bf16[528,128]{1,0:T(8,128)(2,1)}, bf16[528,128]{1,0:T(8,128)(2,1)S(1)}, u32[]{:S(2)}, u32[]{:S(2)}) collective-permute-start(bf16[528,128]{1,0:T(8,128)(2,1)} %get-tuple-element.57), channel_id=1, source_target_pairs={{0,2},{2,0},{4,6},{6,4},{8,10},{10,8},{12,14},{14,12},{1,3},{3,1},... | collective-permute-start | bytes 405512 | tf_op jit(solution)/shard_map/ppermute | solution.py:596
  11.9 6.7 %collective-permute-start.1 = (bf16[528,128]{1,0:T(8,128)(2,1)}, bf16[528,128]{1,0:T(8,128)(2,1)S(1)}, u32[]{:S(2)}, u32[]{:S(2)}) collective-permute-start(bf16[528,128]{1,0:T(8,128)(2,1)} %get-tuple-element.58), channel_id=1, source_target_pairs={{0,4},{2,6},{4,0},{6,2},{8,12},{10,14},{12,8},{14,10},{1,5},{3,7},... | collective-permute-start | bytes 405512 | tf_op jit(solution)/shard_map/ppermute | solution.py:596
  13.5 6.4 %collective-permute-start.2 = (bf16[528,128]{1,0:T(8,128)(2,1)}, bf16[528,128]{1,0:T(8,128)(2,1)S(1)}, u32[]{:S(2)}, u32[]{:S(2)}) collective-permute-start(bf16[528,128]{1,0:T(8,128)(2,1)} %get-tuple-element.59), channel_id=1, source_target_pairs={{0,6},{2,4},{4,2},{6,0},{8,14},{10,12},{12,10},{14,8},{1,7},{3,5},... | collective-permute-start | bytes 405512 | tf_op jit(solution)/shard_map/ppermute | solution.py:596
  16.0 3.8 %copy-start = (bf16[528,128]{1,0:T(8,128)(2,1)S(1)}, bf16[528,128]{1,0:T(8,128)(2,1)}, u32[]{:S(2)}) copy-start(bf16[528,128]{1,0:T(8,128)(2,1)} %get-tuple-element.65.refs_0_) | copy-start | bytes 405508
  16.0 12.4 %copy-start.9 = (bf16[1536,128]{1,0:T(8,128)(2,1)S(1)}, bf16[1536,128]{1,0:T(8,128)(2,1)}, u32[]{:S(2)}) copy-start(bf16[1536,128]{1,0:T(8,128)(2,1)} %get-tuple-element.74) | copy-start | bytes 1179652
  16.3 3.5 %copy-start.3 = (bf16[4,2048,128]{2,1,0:T(8,128)(2,1)}, bf16[4,2048,128]{2,1,0:T(8,128)(2,1)S(1)}, u32[]{:S(2)}) copy-start(bf16[4,2048,128]{2,1,0:T(8,128)(2,1)S(1)} %get-tuple-element.91.refs_8_) | copy-start | bytes 6291460
  20.6 22.1 %collective-permute-start.3 = (bf16[4,128,128]{2,1,0:T(8,128)(2,1)S(1)}, bf16[4,128,128]{2,1,0:T(8,128)(2,1)S(1)}, u32[]{:S(2)}, u32[]{:S(2)}) collective-permute-start(bf16[4,128,128]{2,1,0:T(8,128)(2,1)S(1)} %leave_quad.1), channel_id=1, source_target_pairs={{0,8},{2,10},{4,12},{6,14},{1,9},{3,11},{5,13},{7,15},{16,24},{18,... | collective-permute-start | bytes 393224 | tf_op jit(solution)/shard_map/ppermute | solution.py:627
  25.2 25.6 %copy-start.1 = (bf16[1536,128]{1,0:T(8,128)(2,1)S(1)}, bf16[1536,128]{1,0:T(8,128)(2,1)}, u32[]{:S(2)}) copy-start(bf16[1536,128]{1,0:T(8,128)(2,1)} %get-tuple-element.78.refs_4_) | copy-start | bytes 1179652
  25.2 17.5 %collective-permute-start.4 = (bf16[1536,128]{1,0:T(8,128)(2,1)}, bf16[1536,128]{1,0:T(8,128)(2,1)S(1)}, u32[]{:S(2)}, u32[]{:S(2)}) collective-permute-start(bf16[1536,128]{1,0:T(8,128)(2,1)} %get-tuple-element.72), channel_id=1, source_target_pairs={{0,2},{2,0},{4,6},{6,4},{8,10},{10,8},{12,14},{14,12},{1,3},{3,1},... | collective-permute-start | bytes 1179656 | tf_op jit(solution)/shard_map/ppermute | solution.py:596
  26.8 15.9 %collective-permute-start.5 = (bf16[1536,128]{1,0:T(8,128)(2,1)}, bf16[1536,128]{1,0:T(8,128)(2,1)S(1)}, u32[]{:S(2)}, u32[]{:S(2)}) collective-permute-start(bf16[1536,128]{1,0:T(8,128)(2,1)} %get-tuple-element.73), channel_id=1, source_target_pairs={{0,4},{2,6},{4,0},{6,2},{8,12},{10,14},{12,8},{14,10},{1,5},{3,7},... | collective-permute-start | bytes 1179656 | tf_op jit(solution)/shard_map/ppermute | solution.py:596
  28.4 16.5 %collective-permute-start.6 = (bf16[1536,128]{1,0:T(8,128)(2,1)S(1)}, bf16[1536,128]{1,0:T(8,128)(2,1)S(1)}, u32[]{:S(2)}, u32[]{:S(2)}) collective-permute-start(bf16[1536,128]{1,0:T(8,128)(2,1)S(1)} %copy-done.9), channel_id=1, source_target_pairs={{0,6},{2,4},{4,2},{6,0},{8,14},{10,12},{12,10},{14,8},{1,7},{3,5},... | collective-permute-start | bytes 1179656 | tf_op jit(solution)/shard_map/ppermute | solution.py:596
  42.7 37.1 %copy-start.2 = (s32[2]{0:T(128)S(1)}, s32[2]{0:T(128)}, u32[]{:S(2)}) copy-start(s32[2]{0:T(128)} %get-tuple-element.64.flag_ref) | copy-start | bytes 28
  46.5 34.9 %all-to-all-start.1 = ((bf16[4,4,128,128]{3,2,1,0:T(8,128)(2,1)}), bf16[4,4,128,128]{3,2,1,0:T(8,128)(2,1)S(1)}, u32[]{:S(2)}, u32[]{:S(2)}) async-start(bf16[4,4,128,128]{3,2,1,0:T(8,128)(2,1)} %enter_states.1), calls=%async_computation.1 | async-start | bytes 1048576 | tf_op jit(solution)/shard_map/all_to_all | solution.py:590
  52.2 15.5 %collective-permute-start.10 = (bf16[4,128,128]{2,1,0:T(8,128)(2,1)S(1)}, bf16[4,128,128]{2,1,0:T(8,128)(2,1)S(1)}, u32[]{:S(2)}, u32[]{:S(2)}) collective-permute-start(bf16[4,128,128]{2,1,0:T(8,128)(2,1)S(1)} %get-tuple-element.87), channel_id=1, source_target_pairs={{0,8},{2,10},{4,12},{6,14},{8,0},{10,2},{12,4},{14,6},{1,9},{3,11}... | collective-permute-start | bytes 393224 | tf_op jit(solution)/shard_map/ppermute | solution.py:596
  53.7 20.3 %collective-permute-start.11 = (bf16[4,128,128]{2,1,0:T(8,128)(2,1)S(1)}, bf16[4,128,128]{2,1,0:T(8,128)(2,1)S(1)}, u32[]{:S(2)}, u32[]{:S(2)}) collective-permute-start(bf16[4,128,128]{2,1,0:T(8,128)(2,1)S(1)} %get-tuple-element.88), channel_id=1, source_target_pairs={{0,10},{2,8},{4,14},{6,12},{8,2},{10,0},{12,6},{14,4},{1,11},{3,9}... | collective-permute-start | bytes 393224 | tf_op jit(solution)/shard_map/ppermute | solution.py:596
  56.6 17.4 %collective-permute-start.12 = (bf16[4,128,128]{2,1,0:T(8,128)(2,1)S(1)}, bf16[4,128,128]{2,1,0:T(8,128)(2,1)S(1)}, u32[]{:S(2)}, u32[]{:S(2)}) collective-permute-start(bf16[4,128,128]{2,1,0:T(8,128)(2,1)S(1)} %get-tuple-element.89), channel_id=1, source_target_pairs={{0,12},{2,14},{4,8},{6,10},{8,4},{10,6},{12,0},{14,2},{1,13},{3,15... | collective-permute-start | bytes 393224 | tf_op jit(solution)/shard_map/ppermute | solution.py:596
  59.0 15.0 %collective-permute-start.13 = (bf16[4,128,128]{2,1,0:T(8,128)(2,1)S(1)}, bf16[4,128,128]{2,1,0:T(8,128)(2,1)S(1)}, u32[]{:S(2)}, u32[]{:S(2)}) collective-permute-start(bf16[4,128,128]{2,1,0:T(8,128)(2,1)S(1)} %get-tuple-element.90), channel_id=1, source_target_pairs={{0,14},{2,12},{4,10},{6,8},{8,6},{10,4},{12,2},{14,0},{1,15},{3,13... | collective-permute-start | bytes 393224 | tf_op jit(solution)/shard_map/ppermute | solution.py:596
  59.9 14.1 %collective-permute-start.7 = (bf16[4,128,128]{2,1,0:T(8,128)(2,1)S(1)}, bf16[4,128,128]{2,1,0:T(8,128)(2,1)S(1)}, u32[]{:S(2)}, u32[]{:S(2)}) collective-permute-start(bf16[4,128,128]{2,1,0:T(8,128)(2,1)S(1)} %get-tuple-element.84), channel_id=1, source_target_pairs={{0,2},{2,0},{4,6},{6,4},{8,10},{10,8},{12,14},{14,12},{1,3},{3,1},... | collective-permute-start | bytes 393224 | tf_op jit(solution)/shard_map/ppermute | solution.py:596
  67.7 6.9 %collective-permute-start.8 = (bf16[4,128,128]{2,1,0:T(8,128)(2,1)S(1)}, bf16[4,128,128]{2,1,0:T(8,128)(2,1)S(1)}, u32[]{:S(2)}, u32[]{:S(2)}) collective-permute-start(bf16[4,128,128]{2,1,0:T(8,128)(2,1)S(1)} %get-tuple-element.85), channel_id=1, source_target_pairs={{0,4},{2,6},{4,0},{6,2},{8,12},{10,14},{12,8},{14,10},{1,5},{3,7},... | collective-permute-start | bytes 393224 | tf_op jit(solution)/shard_map/ppermute | solution.py:596
  74.0 5.9 %collective-permute-start.9 = (bf16[4,128,128]{2,1,0:T(8,128)(2,1)S(1)}, bf16[4,128,128]{2,1,0:T(8,128)(2,1)S(1)}, u32[]{:S(2)}, u32[]{:S(2)}) collective-permute-start(bf16[4,128,128]{2,1,0:T(8,128)(2,1)S(1)} %get-tuple-element.86), channel_id=1, source_target_pairs={{0,6},{2,4},{4,2},{6,0},{8,14},{10,12},{12,10},{14,8},{1,7},{3,5},... | collective-permute-start | bytes 393224 | tf_op jit(solution)/shard_map/ppermute | solution.py:596
  81.3 0.9 copy-start.4
